TPU v7x, 128 devices: a whole 4x4x4 slice. The times are simulated.
128 devices in a mesh: island: 4 (over x_hi, core), fsdp: 32 (over y, x_lo, z).
Axes of the slice: x: 4 (x_hi: 2, x_lo: 2; x = x_hi * 2 + x_lo), y: 4, z: 4, core: 2. Of those that a mesh axis runs over, the one named last changes fastest.
Arguments:
- hidden_acts: bfloat16 [114688, 7168], P(('island', 'fsdp')), may hold values from -24 to 24
- output_grads: bfloat16 [114688, 2048], P(('island', 'fsdp')), may hold values from -0.03540039 to 0.03540039
- island_drift: float32 [4, 7168, 2048], P('island', 'fsdp'), may hold values from -6 to 6
- master_weights: float32 [7168, 2048], P('fsdp'), may hold values from -3 to 3
- momentum: float32 [7168, 2048], P('fsdp'), may hold values from -3 to 3
- mixture: int32 [4], replicated, may hold values from 1 to 128
- denominator: int32 [1], replicated, may hold values from 256 to 1024
Outputs:
- new_weights: bfloat16 [7168, 2048], P('fsdp')
- new_momentum: float32 [7168, 2048], P('fsdp')
All inputs are finite; a program needn't handle non-finite values.
Results may differ from a plain program's by a relative error of at most 0.017.
Values may be sent and summed in bfloat16 or wider, within the bound.
No kernel may reach another device: no remote copies, remote signals or barrier semaphores. Data moves between devices by JAX's collectives and lax.ppermute only.
A program may use at most 128 MiB of HBM per device.

v0:
```python
import functools

import jax
import jax.numpy as jnp
import numpy as np
from jax import lax
from jax.experimental import pallas as pl
from jax.experimental.pallas import tpu as pltpu
from jax.sharding import PartitionSpec as P

inner_rate = 0.5
outer_decay = 0.9
outer_rate = 0.7

AXES = ("island", "fsdp")
RING = 4
BLOCKS = 64
COLS = 256
PANELS = 4
PARTS = 3

ORDERS = tuple(
    tuple(((p + k) % 3, 0) for k in range(3)) + ((0, 1), (1, 1), (2, 1)) for p in range(PARTS)
)


def gray(v):
    return v ^ (v >> 1)


def place(axis_values):
    y, z, x, core = axis_values
    return ((x // 2) * 2 + core) * 32 + y * 8 + (x % 2) * 4 + z


def permutation(move):
    pairs = []
    for y in range(RING):
        for z in range(RING):
            for x in range(RING):
                for core in range(2):
                    pairs.append((place((y, z, x, core)), place(move(y, z, x, core))))
    return pairs


def neighbour(axis, bit):
    def move(y, z, x, core):
        at = [y, z, x]
        at[axis] = gray(gray_flip(at[axis], bit ^ core))
        return (*at, core)

    return permutation(move)


def several(axes):
    def move(y, z, x, core):
        at = [y, z, x]
        for axis in axes:
            at[axis] = gray(gray_flip(at[axis], 1 ^ core))
        return (*at, core)

    return permutation(move)


def gray_flip(v, bit):
    return gray(v) ^ (1 << bit)


def swap_core(y, z, x, core):
    return y, z, x, 1 - core


def opposite(y, z, x, core):
    return y, z, x ^ 2, core


def natural(y, z, x_lo, x_hi):
    return ((y * 2 + x_lo) * RING + z) * 2 + x_hi


def relative_blocks(part, core):
    out = []
    for at in range(BLOCKS):
        flips = [0, 0, 0]
        for step, (axis, bit) in enumerate(ORDERS[part]):
            if (at >> (5 - step)) & 1:
                flips[axis] ^= 1 << (bit ^ core)
        y, z, x = flips
        out.append(natural(gray(y), gray(z), gray(x) % 2, gray(x) // 2))
    return out


QUICK = pl.CostEstimate(flops=1, bytes_accessed=1, transcendentals=0)
MODEST = pl.CostEstimate(flops=2 * 10**9, bytes_accessed=1, transcendentals=0)
LONG = pl.CostEstimate(flops=12 * 10**9, bytes_accessed=1, transcendentals=0)


CUT = 3


def transpose_kernel(begin, where, acts, *rest):
    turned, give, buffer, sems, out_sems = rest[-5:]
    count = give.shape[0]
    width = acts.shape[1] // 8

    def load(i):
        rows = pl.ds(pl.multiple_of((begin + i) * 128, 128), 128)
        return pltpu.make_async_copy(acts.at[rows], buffer.at[i], sems.at[i])

    def write(i):
        return pltpu.make_async_copy(turned.at[1, begin + i], give.at[i], out_sems.at[i])

    for i in range(count):
        load(i).start()
    core = where[0]

    @pl.loop(0, count)
    def _(i):
        load(i).wait()
        for j in range(8):
            block = buffer[i, :, j * width : (j + 1) * width].T
            block = block.reshape(4, 2, width // 8, 128)
            for half in range(2):
                turned[half ^ core, begin + i, j * 4 : (j + 1) * 4] = block[:, half]
        write(i).start()

    for i in range(count):
        write(i).wait()


def transposed(acts, where, turned=None):
    tokens, hidden = acts.shape
    shape = (2, tokens // 128, BLOCKS // 2, hidden // BLOCKS, 128)
    part = 0 if turned is None else 1
    begin, count = (CUT, shape[1] - CUT) if part else (0, CUT)
    return pl.pallas_call(
        functools.partial(transpose_kernel, begin),
        in_specs=[pl.BlockSpec(memory_space=pltpu.SMEM), pl.BlockSpec(memory_space=pl.ANY)]
        + [pl.BlockSpec(memory_space=pltpu.VMEM)] * part,
        out_specs=[pl.BlockSpec(memory_space=pltpu.VMEM), pl.BlockSpec(memory_space=pl.ANY)],
        out_shape=[pltpu.VMEM(shape, acts.dtype), pltpu.HBM((count, *shape[2:]), acts.dtype)],
        scratch_shapes=[
            pltpu.VMEM((count, 128, hidden), acts.dtype),
            pltpu.SemaphoreType.DMA((count,)),
            pltpu.SemaphoreType.DMA((count,)),
        ],
        input_output_aliases={2: 0} if part else {},
        compiler_params=pltpu.CompilerParams(vmem_limit_bytes=9 << 20),
        cost_estimate=LONG,
        name=f"transpose_acts_{part}",
    )(where, in_hbm(acts), *([in_vmem(turned)] if part else []))


def weight_of(island, mixture):
    return mixture[island].astype(jnp.float32)


def scale_kernel(where, mixture, grads, other, out, other_out, sems):
    pairs = ((grads, out), (other, other_out))
    copies = [pltpu.make_async_copy(src, dst, sems.at[i]) for i, (src, dst) in enumerate(pairs)]
    for copy in copies:
        copy.start()
    for i, (_, dst) in enumerate(pairs):
        factor = weight_of(where[2] ^ i, mixture)
        copies[i].wait()

        @pl.loop(0, dst.shape[0] // 128)
        def _(k, dst=dst, factor=factor):
            here = pl.ds(pl.multiple_of(k * 128, 128), 128)
            dst[here] = (dst[here].astype(jnp.float32) * factor).astype(dst.dtype)


def scaled(where, mixture, grads, other):
    return pl.pallas_call(
        scale_kernel,
        in_specs=[pl.BlockSpec(memory_space=pltpu.SMEM)] * 2 + [pl.BlockSpec(memory_space=pl.ANY)] * 2,
        out_specs=[pl.BlockSpec(memory_space=pltpu.VMEM)] * 2,
        out_shape=[pltpu.VMEM(grads.shape, grads.dtype)] * 2,
        scratch_shapes=[pltpu.SemaphoreType.DMA((2,))],
        compiler_params=pltpu.CompilerParams(vmem_limit_bytes=4 << 20),
        cost_estimate=pl.CostEstimate(flops=10**11, bytes_accessed=1, transcendentals=0),
        name="scale_grads",
    )(where, mixture, in_hbm(grads), other)


def load_kernel(part, source, *rest):
    out, sem = rest[-2:]
    copy = pltpu.make_async_copy(source, out.at[pl.ds(CUT * part, source.shape[0])], sem)
    copy.start()
    copy.wait()


def loaded(value, panels, out=None):
    part = 0 if out is None else 1
    return pl.pallas_call(
        functools.partial(load_kernel, part),
        in_specs=[pl.BlockSpec(memory_space=pl.ANY)] + [pl.BlockSpec(memory_space=pltpu.VMEM)] * part,
        out_specs=pl.BlockSpec(memory_space=pltpu.VMEM),
        out_shape=pltpu.VMEM((panels, *value.shape[1:]), value.dtype),
        scratch_shapes=[pltpu.SemaphoreType.DMA],
        input_output_aliases={1: 0} if part else {},
        compiler_params=pltpu.CompilerParams(vmem_limit_bytes=2 << 20),
        cost_estimate=QUICK,
        name=f"load_acts_{part}",
    )(value, *([in_vmem(out)] if part else []))


def drift_kernel(where, mixture, drift, mine, theirs, buffer, sems):
    rows = mine.shape[0]
    core = where[0]
    copies = [
        pltpu.make_async_copy(drift.at[0, pl.ds(half * rows, rows)], buffer.at[i], sems.at[i])
        for i, half in enumerate((core, 1 - core))
    ]
    for copy in copies:
        copy.start()
    factor = weight_of(where[2], mixture)
    copies[0].wait()
    mine[...] = buffer[0] * factor
    copies[1].wait()
    theirs[...] = (buffer[1] * factor).astype(theirs.dtype)


def weighted_drift(where, mixture, drift):
    rows, width = drift.shape[1] // 2, drift.shape[2]
    return pl.pallas_call(
        drift_kernel,
        in_specs=[pl.BlockSpec(memory_space=pltpu.SMEM)] * 2 + [pl.BlockSpec(memory_space=pl.ANY)],
        out_specs=[pl.BlockSpec(memory_space=pltpu.VMEM)] * 2,
        out_shape=[
            jax.ShapeDtypeStruct((rows, width), jnp.float32),
            jax.ShapeDtypeStruct((rows, width), jnp.bfloat16),
        ],
        scratch_shapes=[
            pltpu.VMEM((2, rows, width), jnp.float32),
            pltpu.SemaphoreType.DMA((2,)),
        ],
        compiler_params=pltpu.CompilerParams(vmem_limit_bytes=6 << 20),
        cost_estimate=QUICK,
        name="weigh_drift",
    )(where, mixture, in_hbm(drift))


def drift_add_kernel(where, mine, received, mine_out, theirs_out):
    half = mine_out.shape[1]
    first = where[3] == 0
    total_left = mine[:, :half] + received[:, :half].astype(jnp.float32)
    total_right = mine[:, half:] + received[:, half:].astype(jnp.float32)
    mine_out[...] = jnp.where(first, total_left, total_right)
    theirs_out[...] = jnp.where(first, total_right, total_left).astype(theirs_out.dtype)


def added_drift(where, mine, received):
    rows, width = mine.shape
    return pl.pallas_call(
        drift_add_kernel,
        in_specs=[pl.BlockSpec(memory_space=pltpu.SMEM)]
        + [pl.BlockSpec(memory_space=pltpu.VMEM)] * 2,
        out_specs=[pl.BlockSpec(memory_space=pltpu.VMEM)] * 2,
        out_shape=[
            jax.ShapeDtypeStruct((rows, width // 2), jnp.float32),
            jax.ShapeDtypeStruct((rows, width // 2), jnp.bfloat16),
        ],
        compiler_params=pltpu.CompilerParams(vmem_limit_bytes=6 << 20),
        cost_estimate=QUICK,
        name="add_drift",
    )(where, mine, received)


def panel_kernel(first, part, offsets, where, *rest):
    count = len(rest) - 1 - len(offsets)
    pairs, more, out = rest[:count], rest[count:-1], rest[-1]
    acts, grads = pairs[: count // 2], pairs[count // 2 :]
    acts = [ref.at[0] if len(ref.shape) == 5 else ref for ref in acts]
    row_lo, row_n = SHARED_ROWS[part]
    rows = acts[0].shape[2]
    orders = [relative_blocks(part, core) for core in range(2)]

    def relative(position):
        return jnp.where(where[0] == 0, orders[0][position], orders[1][position])

    split = TILE if part == 0 else out.shape[0]
    size = split // 2

    def blocks(low, tile):
        base = where[1] ^ (low * relative(1)) ^ (tile * relative(TILE))
        at = [tile * TILE + low + 2 * k for k in range(size)]
        picks = [(base ^ relative(first + 2 * k)) >> 1 for k in range(size)]
        edge = pl.multiple_of(((base ^ relative(first)) & 1) * (PANELS * COLS), COLS)

        def left(lo, n):
            return jnp.concatenate(
                [
                    jnp.concatenate(
                        [ref[i, k, lo : lo + n] for ref in acts for i in range(ref.shape[0])],
                        axis=1,
                    )
                    for k in picks
                ],
                axis=0,
            )

        def right(panel):
            lanes = pl.ds(edge + panel * COLS, COLS)
            return jnp.concatenate([ref[:, lanes] for ref in grads], axis=0)

        main = jnp.dot(left(0, rows), right(part), preferred_element_type=jnp.float32)
        shared = jnp.dot(left(row_lo, row_n), right(PARTS), preferred_element_type=jnp.float32)
        main = main.reshape(size, rows, COLS)
        shared = shared.reshape(size, row_n, COLS)
        for i, k in enumerate(at):
            top, bottom = main[i], shared[i]
            for ref, offset in zip(more, offsets):
                top = top + ref[offset + k, :rows].astype(jnp.float32)
                bottom = bottom + ref[offset + k, rows:].astype(jnp.float32)
            out[k, :rows] = top.astype(out.dtype)
            out[k, rows:] = bottom.astype(out.dtype)

    if part == 0:

        @pl.loop(0, out.shape[0] // TILE)
        def _(tile):
            for low in range(2):
                blocks(low, tile)

    else:

        @pl.loop(0, 2)
        def _(low):
            blocks(low, 0)


SHARED_ROWS = ((0, 48), (48, 32), (80, 32))
TILE = 8


def in_hbm(value):
    return pltpu.with_memory_space_constraint(value, pltpu.HBM)


def in_vmem(value):
    return pltpu.with_memory_space_constraint(value, pltpu.VMEM)


def panel(operands, where, part, first, count, received, dtype=jnp.bfloat16):
    height = operands[0].shape[-2] + SHARED_ROWS[part][1]
    return pl.pallas_call(
        functools.partial(panel_kernel, first, part, tuple(offset for _, offset in received)),
        in_specs=[pl.BlockSpec(memory_space=pltpu.SMEM)]
        + [pl.BlockSpec(memory_space=pltpu.VMEM)] * (len(operands) + len(received)),
        out_specs=pl.BlockSpec(memory_space=pltpu.VMEM),
        out_shape=jax.ShapeDtypeStruct((count, height, COLS), dtype),
        compiler_params=pltpu.CompilerParams(vmem_limit_bytes=9 << 20),
        cost_estimate=MODEST,
        name=f"panel_{part}_{first}_{len(operands)}_{len(received)}",
    )(where, *[in_vmem(v) for v in operands], *[v for v, _ in received])


def load_state_kernel(master, moment, master_out, moment_out, sems):
    copies = [
        pltpu.make_async_copy(src, dst, sems.at[i])
        for i, (src, dst) in enumerate(((master, master_out), (moment, moment_out)))
    ]
    for copy in copies:
        copy.start()
    for copy in copies:
        copy.wait()


def loaded_state(master, moment):
    return pl.pallas_call(
        load_state_kernel,
        in_specs=[pl.BlockSpec(memory_space=pl.ANY)] * 2,
        out_specs=[pl.BlockSpec(memory_space=pltpu.VMEM)] * 2,
        out_shape=[pltpu.VMEM(master.shape, master.dtype)] * 2,
        scratch_shapes=[pltpu.SemaphoreType.DMA((2,))],
        compiler_params=pltpu.CompilerParams(vmem_limit_bytes=2 << 20),
        cost_estimate=QUICK,
        name="load_state",
    )(in_hbm(master), in_hbm(moment))


def combine_kernel(where, denominator, own, own_rest, far_own, far_rest, out):
    rows = out.shape[0]
    divisor = denominator[0].astype(jnp.float32)
    first = where[3] == 0

    def combined(a, b):
        total = a.astype(jnp.float32) + b.astype(jnp.float32)
        return (inner_rate * total / divisor).astype(out.dtype)

    at = 0
    width = PANELS * COLS
    for part, (lo, n) in enumerate(SHARED_ROWS):
        for start, count, row, col in ((at, rows, 0, part), (at + rows, n, lo, PARTS)):
            here = slice(start, start + count)
            mine = combined(own[here], own_rest[here])
            far = combined(far_own[here], far_rest[here])
            for half in range(2):
                lanes = slice(half * width + col * COLS, half * width + (col + 1) * COLS)
                value = jnp.where(first, mine, far) if half == 0 else jnp.where(first, far, mine)
                out[row : row + count, lanes] = value
        at += rows + n


def combine(where, denominator, rows, *sums):
    return pl.pallas_call(
        combine_kernel,
        in_specs=[pl.BlockSpec(memory_space=pltpu.SMEM)] * 2 + [pl.BlockSpec(memory_space=pltpu.VMEM)] * 4,
        out_specs=pl.BlockSpec(memory_space=pltpu.VMEM),
        out_shape=jax.ShapeDtypeStruct((rows, 2 * PANELS * COLS), jnp.bfloat16),
        compiler_params=pltpu.CompilerParams(vmem_limit_bytes=6 << 20),
        cost_estimate=QUICK,
        name="combine",
    )(where, denominator, *sums)


def update_kernel(where, mine, theirs, master, moment, weights_out, moment_out, weights, moments, sems):
    rows = mine.shape[0]
    first = where[0] == 0
    copies = []
    for half in range(2):
        here = slice(half * rows, (half + 1) * rows)
        a, b = (mine, theirs) if half == 0 else (theirs, mine)
        combined = jnp.where(first, a[...], b[...]).astype(jnp.float32)
        new_moment = outer_decay * moment[here] + combined
        new_master = master[here] - outer_rate * (combined + outer_decay * new_moment)
        weights[here] = new_master.astype(weights.dtype)
        moments[here] = new_moment
        for i, (src, dst) in enumerate(((weights, weights_out), (moments, moment_out))):
            there = pl.ds(half * rows, rows)
            copies.append(pltpu.make_async_copy(src.at[there], dst.at[there], sems.at[half, i]))
            copies[-1].start()
    for copy in copies:
        copy.wait()


def update(where, mine, theirs, master, moment):
    shape = master.shape
    return pl.pallas_call(
        update_kernel,
        in_specs=[pl.BlockSpec(memory_space=pltpu.SMEM)] + [pl.BlockSpec(memory_space=pltpu.VMEM)] * 4,
        out_specs=[pl.BlockSpec(memory_space=pl.ANY)] * 2,
        out_shape=[
            jax.ShapeDtypeStruct(shape, jnp.bfloat16),
            jax.ShapeDtypeStruct(shape, jnp.float32),
        ],
        scratch_shapes=[
            pltpu.VMEM(shape, jnp.bfloat16),
            pltpu.VMEM(shape, jnp.float32),
            pltpu.SemaphoreType.DMA((2, 2)),
        ],
        compiler_params=pltpu.CompilerParams(vmem_limit_bytes=10 << 20),
        cost_estimate=QUICK,
        name="update",
    )(where, mine, theirs, in_vmem(master), in_vmem(moment))


def send(value, pairs):
    return lax.ppermute(value, AXES, pairs)


def total(terms):
    out = terms[0].astype(jnp.float32)
    for term in terms[1:]:
        out = out + term.astype(jnp.float32)
    return out


def after(value, *others):
    return lax.optimization_barrier((value, others))[0]


def stacked(block):
    pieces = []
    for part, (lo, n) in enumerate(SHARED_ROWS):
        pieces.append(block[:, part * COLS : (part + 1) * COLS])
        pieces.append(block[lo : lo + n, PARTS * COLS :])
    return jnp.concatenate(pieces, axis=0)


def rounded(value):
    return lax.reduce_precision(value, 8, 7).astype(jnp.bfloat16)


def body(hidden_acts, output_grads, island_drift, master_weights, momentum, mixture, denominator):
    island = lax.axis_index("island")
    fsdp = lax.axis_index("fsdp")
    x_hi = island // 2
    own_place = natural(fsdp // 8, fsdp % 4, (fsdp // 4) % 2, x_hi)
    where = jnp.stack([island % 2, own_place, island, x_hi]).astype(jnp.int32)
    swap = permutation(swap_core)

    other_grads = send(output_grads, swap)
    turned, give = transposed(hidden_acts, where)
    gives = [send(give, swap)]
    turned, give = transposed(hidden_acts, where, turned)
    gives.append(send(give, swap))
    where, turned = lax.optimization_barrier((where, turned))
    grads, other_grads = scaled(where, mixture, output_grads, other_grads)
    last = [grads]

    def product(operands, p, *args):
        out = panel(operands, after(where, *last), p, *args)
        last[:] = [out]
        return out

    early = [product((turned, grads), p, 48, 16, (), jnp.float32) for p in range(2)]
    gives[0], _ = lax.optimization_barrier((gives[0], last[0]))
    other = loaded(gives[0], turned.shape[1])
    gives[1], other = lax.optimization_barrier((gives[1], other))
    other = loaded(gives[1], turned.shape[1], other)
    operands = (turned, other, grads, other_grads)
    last = [other]

    def chunk(first, count, received):
        return [product(operands, p, first, count, received[p]) for p in range(PARTS)]

    def step(k, values):
        return [send(values[p], neighbour(*ORDERS[p][k])) for p in range(PARTS)]

    far = [product((other, other_grads), p, 48, 16, ((v, 0),)) for p, v in enumerate(early)]
    far.append(product(operands, 2, 48, 16, ()))
    got_far = step(0, far)
    got_near = step(0, chunk(32, 16, [()] * PARTS))
    got = step(1, chunk(16, 16, [((v, 0),) for v in got_far]))
    local = chunk(0, 8, [((v, 0),) for v in got_near])

    mine, theirs = weighted_drift(where, mixture, after(island_drift, *last))
    drift_near = send(theirs, swap)
    last = [mine]
    out = []
    for p in range(PARTS):
        out.append(product(operands, p, 8, 8, ((got_near[p], 8), (got[p], 8))))
        if p == 0:
            mine, theirs = added_drift(where, after(mine, *last), drift_near)
            last = [mine]
    third = step(2, out)
    rows = mine.shape[0]
    *third, theirs = lax.optimization_barrier((*third, theirs))
    drift_far = send(theirs, permutation(opposite))

    terms = [
        jnp.concatenate([part[:8] for part in parts], axis=1) for parts in (local, got, third)
    ]
    eight = total(terms)

    ready = eight[2:].astype(jnp.bfloat16)
    arrived = [
        send(ready[2 * k : 2 * k + 2], several(bits))
        for k, bits in ((2, (0, 1)), (1, (0,)), (0, (1,)))
    ]
    master, moment, theirs = lax.optimization_barrier((master_weights, momentum, ready))
    master, moment = loaded_state(master, moment)
    *arrived, drift_far, master = lax.optimization_barrier((*arrived, drift_far, master))
    two = total([eight[:2]] + list(arrived))
    drift_sum = stacked(mine + drift_far.astype(jnp.float32)) * (1.0 / inner_rate)
    own, beside = lax.optimization_barrier((rounded(two[0] + drift_sum), rounded(two[1])))
    own, own_rest, far_own, far_rest = lax.optimization_barrier(
        (
            own,
            send(beside, neighbour(2, 1)),
            send(own, permutation(opposite)),
            send(beside, neighbour(2, 0)),
        )
    )
    half = combine(where, denominator, rows, own, own_rest, far_own, far_rest)
    return update(where, half, send(half, swap), master, moment)


def solution(mesh):
    in_specs = (
        P(("island", "fsdp"), None),
        P(("island", "fsdp"), None),
        P("island", "fsdp", None),
        P("fsdp", None),
        P("fsdp", None),
        P(),
        P(),
    )
    out_specs = (P("fsdp", None), P("fsdp", None))
    return jax.shard_map(body, mesh=mesh, in_specs=in_specs, out_specs=out_specs, check_vma=False)
```

profile of v0, /device:TPU:1, one launch (start us, length us, event | category | flops | bytes accessed | tf_op | source)
XLA Modules:
  0.0 129.9 jit_solution(956683999742870996)
XLA Ops:
  0.6 1.5 %collective-permute-start.2 = (bf16[896,2048]{1,0:T(8,128)(2,1)}, bf16[896,2048]{1,0:T(8,128)(2,1)}, u32[]{:S(2)}, u32[]{:S(2)}) collective-permute-start(bf16[896,2048]{1,0:T(8,128)(2,1)} %grads.1), channel_id=1, source_target_pairs={{0,32},{32,0},{4,36},{36,4},{64,96},{96,64},{68,100},{100,68},{1,3... | collective-permute-start | bytes 11010056 | tf_op jit(solution)/shard_map/ppermute | solution.py:460
  2.1 0.1 pad_add_fusion.where
  2.2 4.7 %transpose_acts_0.1 = (bf16[2,7,32,112,128]{4,3,2,1,0:T(8,128)(2,1)S(1)}, bf16[3,32,112,128]{3,2,1,0:T(8,128)(2,1)}) custom-call(s32[4]{0:T(128)S(1)} %pad_add_fusion.where, bf16[896,7168]{1,0:T(8,128)(2,1)} %acts.3), custom_call_target="tpu_custom_call" | custom-call | flops 12000000000 | bytes 1 | tf_op jit(solution)/shard_map/transpose_acts_0/pallas_call | solution.py:136
  6.9 0.2 collective-permute-start.1
  7.1 5.5 %transpose_acts_1.1 = (bf16[2,7,32,112,128]{4,3,2,1,0:T(8,128)(2,1)S(1)}, bf16[4,32,112,128]{3,2,1,0:T(8,128)(2,1)}) custom-call(s32[4]{0:T(128)S(1)} %pad_add_fusion.where, bf16[896,7168]{1,0:T(8,128)(2,1)} %acts.3, bf16[2,7,32,112,128]{4,3,2,1,0:T(8,128)(2,1)S(1)} %get-tuple-element.55.rest_0_), custom_call_target="tpu_custom_call", output_to_operand_aliasing={{0}: (2, {})} | custom-call | flops 12000000000 | bytes 1 | tf_op jit(solution)/shard_map/transpose_acts_1/pallas_call | solution.py:136
  12.5 0.5 collective-permute-start
  13.0 4.3 %scale_grads.1 = (bf16[896,2048]{1,0:T(8,128)(2,1)S(1)}, bf16[896,2048]{1,0:T(8,128)(2,1)S(1)}) custom-call(s32[4]{0:T(128)S(1)} %pad_add_fusion.where, s32[4]{0:T(128)S(1)} %copy-done.1, bf16[896,2048]{1,0:T(8,128)(2,1)} %grads.1, bf16[896,2048]{1,0:T(8,128)(2,1)} %collective-permute-done.2.other), custom_call_target="tpu_custom_call" | custom-call | flops 99999997952 | bytes 1 | tf_op jit(solution)/shard_map/scale_grads/pallas_call | solution.py:174
  17.4 2.3 %panel_0_48_2_0.1.rest_2_ = f32[16,160,256]{2,1,0:T(8,128)S(1)} custom-call(s32[4]{0:T(128)S(1)} %pad_add_fusion.where, bf16[2,7,32,112,128]{4,3,2,1,0:T(8,128)(2,1)S(1)} %get-tuple-element.62.rest_0_, bf16[896,2048]{1,0:T(8,128)(2,1)S(1)} %get-tuple-element.60.rest_1_.rest_2_), custom_call_target="tpu_custom_call" | custom-call | flops 2000000000 | bytes 1 | tf_op jit(solution)/shard_map/panel_0_48_2_0/pallas_call | solution.py:347
  19.7 2.2 %panel_1_48_2_0.1.rest_2_ = f32[16,144,256]{2,1,0:T(8,128)S(1)} custom-call(s32[4]{0:T(128)S(1)} %pad_add_fusion.where, bf16[2,7,32,112,128]{4,3,2,1,0:T(8,128)(2,1)S(1)} %get-tuple-element.62.rest_0_, bf16[896,2048]{1,0:T(8,128)(2,1)S(1)} %get-tuple-element.60.rest_1_.rest_2_), custom_call_target="tpu_custom_call" | custom-call | flops 2000000000 | bytes 1 | tf_op jit(solution)/shard_map/panel_1_48_2_0/pallas_call | solution.py:347
  21.8 0.4 load_acts_0.1.rest_0_
  22.2 0.3 load_acts_1.1.rest_0_.rest_1_
  22.5 2.3 %panel_0_48_2_1.1 = bf16[16,160,256]{2,1,0:T(8,128)(2,1)S(1)} custom-call(s32[4]{0:T(128)S(1)} %pad_add_fusion.where, bf16[7,32,112,128]{3,2,1,0:T(8,128)(2,1)S(1)} %load_acts_1.1.rest_0_.rest_1_, bf16[896,2048]{1,0:T(8,128)(2,1)S(1)} %get-tuple-element.68.rest_1_.rest_3_, f32[16,160,256]{2,1,0:T(8,128)S(1)} %panel_0_48_2_0.1.rest_2_), custom_call_target="tpu_custom_call" | custom-call | flops 2000000000 | bytes 1 | tf_op jit(solution)/shard_map/panel_0_48_2_1/pallas_call | solution.py:347
  24.8 2.9 %collective-permute-start.3 = (bf16[16,160,256]{2,1,0:T(8,128)(2,1)S(1)}, bf16[16,160,256]{2,1,0:T(8,128)(2,1)S(1)}, u32[]{:S(2)}, u32[]{:S(2)}) collective-permute-start(bf16[16,160,256]{2,1,0:T(8,128)(2,1)S(1)} %panel_0_48_2_1.1), channel_id=1, source_target_pairs={{0,8},{32,56},{4,12},{36,60},{64,72},{96,120},{68,76},{100,124},{1... | collective-permute-start | bytes 3932168 | tf_op jit(solution)/shard_map/ppermute | solution.py:460
  27.7 2.2 %panel_1_48_2_1.1 = bf16[16,144,256]{2,1,0:T(8,128)(2,1)S(1)} custom-call(s32[4]{0:T(128)S(1)} %pad_add_fusion.where, bf16[7,32,112,128]{3,2,1,0:T(8,128)(2,1)S(1)} %load_acts_1.1.rest_0_.rest_1_, bf16[896,2048]{1,0:T(8,128)(2,1)S(1)} %get-tuple-element.68.rest_1_.rest_3_, f32[16,144,256]{2,1,0:T(8,128)S(1)} %panel_1_48_2_0.1.rest_2_), custom_call_target="tpu_custom_call" | custom-call | flops 2000000000 | bytes 1 | tf_op jit(solution)/shard_map/panel_1_48_2_1/pallas_call | solution.py:347
  29.9 3.8 %collective-permute-start.4 = (bf16[16,144,256]{2,1,0:T(8,128)(2,1)S(1)}, bf16[16,144,256]{2,1,0:T(8,128)(2,1)S(1)}, u32[]{:S(2)}, u32[]{:S(2)}) collective-permute-start(bf16[16,144,256]{2,1,0:T(8,128)(2,1)S(1)} %panel_1_48_2_1.1), channel_id=1, source_target_pairs={{0,1},{32,35},{4,5},{36,39},{64,65},{96,99},{68,69},{100,103},{1,0... | collective-permute-start | bytes 3538952 | tf_op jit(solution)/shard_map/ppermute | solution.py:460
  33.7 3.1 %panel_2_48_4_0.1 = bf16[16,144,256]{2,1,0:T(8,128)(2,1)S(1)} custom-call(s32[4]{0:T(128)S(1)} %pad_add_fusion.where, bf16[2,7,32,112,128]{4,3,2,1,0:T(8,128)(2,1)S(1)} %get-tuple-element.62.rest_0_, bf16[7,32,112,128]{3,2,1,0:T(8,128)(2,1)S(1)} %load_acts_1.1.rest_0_.rest_1_, bf16[896,2048]{1,0:T(8,128)(2,1)S(1)} %get-tuple-element.60.rest_1_.rest_2_, ...), custom_call_target="tpu_custom_call" | custom-call | flops 2000000000 | bytes 1 | tf_op jit(solution)/shard_map/panel_2_48_4_0/pallas_call | solution.py:347
  36.7 2.6 %collective-permute-start.5 = (bf16[16,144,256]{2,1,0:T(8,128)(2,1)S(1)}, bf16[16,144,256]{2,1,0:T(8,128)(2,1)S(1)}, u32[]{:S(2)}, u32[]{:S(2)}) collective-permute-start(bf16[16,144,256]{2,1,0:T(8,128)(2,1)S(1)} %panel_2_48_4_0.1), channel_id=1, source_target_pairs={{0,4},{32,100},{4,0},{36,96},{64,68},{96,36},{68,64},{100,32},{1,5... | collective-permute-start | bytes 3538952 | tf_op jit(solution)/shard_map/ppermute | solution.py:460
  39.3 3.3 %panel_0_32_4_0.1 = bf16[16,160,256]{2,1,0:T(8,128)(2,1)S(1)} custom-call(s32[4]{0:T(128)S(1)} %pad_add_fusion.where, bf16[2,7,32,112,128]{4,3,2,1,0:T(8,128)(2,1)S(1)} %get-tuple-element.62.rest_0_, bf16[7,32,112,128]{3,2,1,0:T(8,128)(2,1)S(1)} %load_acts_1.1.rest_0_.rest_1_, bf16[896,2048]{1,0:T(8,128)(2,1)S(1)} %get-tuple-element.60.rest_1_.rest_2_, ...), custom_call_target="tpu_custom_call" | custom-call | flops 2000000000 | bytes 1 | tf_op jit(solution)/shard_map/panel_0_32_4_0/pallas_call | solution.py:347
  42.6 0.1 collective-permute-start.6
  42.7 3.1 %panel_1_32_4_0.1 = bf16[16,144,256]{2,1,0:T(8,128)(2,1)S(1)} custom-call(s32[4]{0:T(128)S(1)} %pad_add_fusion.where, bf16[2,7,32,112,128]{4,3,2,1,0:T(8,128)(2,1)S(1)} %get-tuple-element.62.rest_0_, bf16[7,32,112,128]{3,2,1,0:T(8,128)(2,1)S(1)} %load_acts_1.1.rest_0_.rest_1_, bf16[896,2048]{1,0:T(8,128)(2,1)S(1)} %get-tuple-element.60.rest_1_.rest_2_, ...), custom_call_target="tpu_custom_call" | custom-call | flops 2000000000 | bytes 1 | tf_op jit(solution)/shard_map/panel_1_32_4_0/pallas_call | solution.py:347
  45.8 0.2 collective-permute-start.7
  46.0 3.1 %panel_2_32_4_0.1 = bf16[16,144,256]{2,1,0:T(8,128)(2,1)S(1)} custom-call(s32[4]{0:T(128)S(1)} %pad_add_fusion.where, bf16[2,7,32,112,128]{4,3,2,1,0:T(8,128)(2,1)S(1)} %get-tuple-element.62.rest_0_, bf16[7,32,112,128]{3,2,1,0:T(8,128)(2,1)S(1)} %load_acts_1.1.rest_0_.rest_1_, bf16[896,2048]{1,0:T(8,128)(2,1)S(1)} %get-tuple-element.60.rest_1_.rest_2_, ...), custom_call_target="tpu_custom_call" | custom-call | flops 2000000000 | bytes 1 | tf_op jit(solution)/shard_map/panel_2_32_4_0/pallas_call | solution.py:347
  49.1 0.5 collective-permute-start.8
  49.5 3.4 %panel_0_16_4_1.1 = bf16[16,160,256]{2,1,0:T(8,128)(2,1)S(1)} custom-call(s32[4]{0:T(128)S(1)} %pad_add_fusion.where, bf16[2,7,32,112,128]{4,3,2,1,0:T(8,128)(2,1)S(1)} %get-tuple-element.62.rest_0_, bf16[7,32,112,128]{3,2,1,0:T(8,128)(2,1)S(1)} %load_acts_1.1.rest_0_.rest_1_, bf16[896,2048]{1,0:T(8,128)(2,1)S(1)} %get-tuple-element.60.rest_1_.rest_2_, ...), custom_call_target="tpu_custom_call" | custom-call | flops 2000000000 | bytes 1 | tf_op jit(solution)/shard_map/panel_0_16_4_1/pallas_call | solution.py:347
  52.9 2.6 %collective-permute-start.9 = (bf16[16,160,256]{2,1,0:T(8,128)(2,1)S(1)}, bf16[16,160,256]{2,1,0:T(8,128)(2,1)S(1)}, u32[]{:S(2)}, u32[]{:S(2)}) collective-permute-start(bf16[16,160,256]{2,1,0:T(8,128)(2,1)S(1)} %panel_0_16_4_1.1), channel_id=1, source_target_pairs={{0,1},{32,35},{4,5},{36,39},{64,65},{96,99},{68,69},{100,103},{1,0... | collective-permute-start | bytes 3932168 | tf_op jit(solution)/shard_map/ppermute | solution.py:460
  55.6 3.1 %panel_1_16_4_1.1 = bf16[16,144,256]{2,1,0:T(8,128)(2,1)S(1)} custom-call(s32[4]{0:T(128)S(1)} %pad_add_fusion.where, bf16[2,7,32,112,128]{4,3,2,1,0:T(8,128)(2,1)S(1)} %get-tuple-element.62.rest_0_, bf16[7,32,112,128]{3,2,1,0:T(8,128)(2,1)S(1)} %load_acts_1.1.rest_0_.rest_1_, bf16[896,2048]{1,0:T(8,128)(2,1)S(1)} %get-tuple-element.60.rest_1_.rest_2_, ...), custom_call_target="tpu_custom_call" | custom-call | flops 2000000000 | bytes 1 | tf_op jit(solution)/shard_map/panel_1_16_4_1/pallas_call | solution.py:347
  58.7 2.6 %collective-permute-start.10 = (bf16[16,144,256]{2,1,0:T(8,128)(2,1)S(1)}, bf16[16,144,256]{2,1,0:T(8,128)(2,1)S(1)}, u32[]{:S(2)}, u32[]{:S(2)}) collective-permute-start(bf16[16,144,256]{2,1,0:T(8,128)(2,1)S(1)} %panel_1_16_4_1.1), channel_id=1, source_target_pairs={{0,4},{32,100},{4,0},{36,96},{64,68},{96,36},{68,64},{100,32},{1,5... | collective-permute-start | bytes 3538952 | tf_op jit(solution)/shard_map/ppermute | solution.py:460
  61.2 3.1 %panel_2_16_4_1.1 = bf16[16,144,256]{2,1,0:T(8,128)(2,1)S(1)} custom-call(s32[4]{0:T(128)S(1)} %pad_add_fusion.where, bf16[2,7,32,112,128]{4,3,2,1,0:T(8,128)(2,1)S(1)} %get-tuple-element.62.rest_0_, bf16[7,32,112,128]{3,2,1,0:T(8,128)(2,1)S(1)} %load_acts_1.1.rest_0_.rest_1_, bf16[896,2048]{1,0:T(8,128)(2,1)S(1)} %get-tuple-element.60.rest_1_.rest_2_, ...), custom_call_target="tpu_custom_call" | custom-call | flops 2000000000 | bytes 1 | tf_op jit(solution)/shard_map/panel_2_16_4_1/pallas_call | solution.py:347
  64.3 2.7 %collective-permute-start.11 = (bf16[16,144,256]{2,1,0:T(8,128)(2,1)S(1)}, bf16[16,144,256]{2,1,0:T(8,128)(2,1)S(1)}, u32[]{:S(2)}, u32[]{:S(2)}) collective-permute-start(bf16[16,144,256]{2,1,0:T(8,128)(2,1)S(1)} %panel_2_16_4_1.1), channel_id=1, source_target_pairs={{0,8},{32,56},{4,12},{36,60},{64,72},{96,120},{68,76},{100,124},{1... | collective-permute-start | bytes 3538952 | tf_op jit(solution)/shard_map/ppermute | solution.py:460
  67.1 1.9 %panel_0_0_4_1.1 = bf16[8,160,256]{2,1,0:T(8,128)(2,1)S(1)} custom-call(s32[4]{0:T(128)S(1)} %pad_add_fusion.where, bf16[2,7,32,112,128]{4,3,2,1,0:T(8,128)(2,1)S(1)} %get-tuple-element.62.rest_0_, bf16[7,32,112,128]{3,2,1,0:T(8,128)(2,1)S(1)} %load_acts_1.1.rest_0_.rest_1_, bf16[896,2048]{1,0:T(8,128)(2,1)S(1)} %get-tuple-element.60.rest_1_.rest_2_, ...), custom_call_target="tpu_custom_call" | custom-call | flops 2000000000 | bytes 1 | tf_op jit(solution)/shard_map/panel_0_0_4_1/pallas_call | solution.py:347
  69.0 2.0 %panel_1_0_4_1.1 = bf16[8,144,256]{2,1,0:T(8,128)(2,1)S(1)} custom-call(s32[4]{0:T(128)S(1)} %pad_add_fusion.where, bf16[2,7,32,112,128]{4,3,2,1,0:T(8,128)(2,1)S(1)} %get-tuple-element.62.rest_0_, bf16[7,32,112,128]{3,2,1,0:T(8,128)(2,1)S(1)} %load_acts_1.1.rest_0_.rest_1_, bf16[896,2048]{1,0:T(8,128)(2,1)S(1)} %get-tuple-element.60.rest_1_.rest_2_, ...), custom_call_target="tpu_custom_call" | custom-call | flops 2000000000 | bytes 1 | tf_op jit(solution)/shard_map/panel_1_0_4_1/pallas_call | solution.py:347
  71.1 2.0 %panel_2_0_4_1.1 = bf16[8,144,256]{2,1,0:T(8,128)(2,1)S(1)} custom-call(s32[4]{0:T(128)S(1)} %pad_add_fusion.where, bf16[2,7,32,112,128]{4,3,2,1,0:T(8,128)(2,1)S(1)} %get-tuple-element.62.rest_0_, bf16[7,32,112,128]{3,2,1,0:T(8,128)(2,1)S(1)} %load_acts_1.1.rest_0_.rest_1_, bf16[896,2048]{1,0:T(8,128)(2,1)S(1)} %get-tuple-element.60.rest_1_.rest_2_, ...), custom_call_target="tpu_custom_call" | custom-call | flops 2000000000 | bytes 1 | tf_op jit(solution)/shard_map/panel_2_0_4_1/pallas_call | solution.py:347
  73.1 2.1 %weigh_drift.1 = (f32[112,2048]{1,0:T(8,128)S(1)}, bf16[112,2048]{1,0:T(8,128)(2,1)S(1)}) custom-call(s32[4]{0:T(128)S(1)} %pad_add_fusion.where, s32[4]{0:T(128)S(1)} %copy-done.1, f32[1,224,2048]{2,1,0:T(8,128)} %drift), custom_call_target="tpu_custom_call" | custom-call | flops 1 | bytes 1 | tf_op jit(solution)/shard_map/weigh_drift/pallas_call | solution.py:226
  75.1 0.1 collective-permute-start.13
  75.2 1.0 collective-permute-done.9.rest_5_
  76.2 2.0 %panel_0_8_4_2.1 = bf16[8,160,256]{2,1,0:T(8,128)(2,1)S(1)} custom-call(s32[4]{0:T(128)S(1)} %pad_add_fusion.where, bf16[2,7,32,112,128]{4,3,2,1,0:T(8,128)(2,1)S(1)} %get-tuple-element.62.rest_0_, bf16[7,32,112,128]{3,2,1,0:T(8,128)(2,1)S(1)} %load_acts_1.1.rest_0_.rest_1_, bf16[896,2048]{1,0:T(8,128)(2,1)S(1)} %get-tuple-element.60.rest_1_.rest_2_, ...), custom_call_target="tpu_custom_call" | custom-call | flops 2000000000 | bytes 1 | tf_op jit(solution)/shard_map/panel_0_8_4_2/pallas_call | solution.py:347
  78.2 0.3 collective-permute-start.12
  78.5 0.7 add_drift.1
  79.2 2.0 %panel_1_8_4_2.1 = bf16[8,144,256]{2,1,0:T(8,128)(2,1)S(1)} custom-call(s32[4]{0:T(128)S(1)} %pad_add_fusion.where, bf16[2,7,32,112,128]{4,3,2,1,0:T(8,128)(2,1)S(1)} %get-tuple-element.62.rest_0_, bf16[7,32,112,128]{3,2,1,0:T(8,128)(2,1)S(1)} %load_acts_1.1.rest_0_.rest_1_, bf16[896,2048]{1,0:T(8,128)(2,1)S(1)} %get-tuple-element.60.rest_1_.rest_2_, ...), custom_call_target="tpu_custom_call" | custom-call | flops 2000000000 | bytes 1 | tf_op jit(solution)/shard_map/panel_1_8_4_2/pallas_call | solution.py:347
  81.2 2.0 %panel_2_8_4_2.1 = bf16[8,144,256]{2,1,0:T(8,128)(2,1)S(1)} custom-call(s32[4]{0:T(128)S(1)} %pad_add_fusion.where, bf16[2,7,32,112,128]{4,3,2,1,0:T(8,128)(2,1)S(1)} %get-tuple-element.62.rest_0_, bf16[7,32,112,128]{3,2,1,0:T(8,128)(2,1)S(1)} %load_acts_1.1.rest_0_.rest_1_, bf16[896,2048]{1,0:T(8,128)(2,1)S(1)} %get-tuple-element.60.rest_1_.rest_2_, ...), custom_call_target="tpu_custom_call" | custom-call | flops 2000000000 | bytes 1 | tf_op jit(solution)/shard_map/panel_2_8_4_2/pallas_call | solution.py:347
  83.3 2.7 %collective-permute-start.15 = (bf16[8,144,256]{2,1,0:T(8,128)(2,1)S(1)}, bf16[8,144,256]{2,1,0:T(8,128)(2,1)S(1)}, u32[]{:S(2)}, u32[]{:S(2)}) collective-permute-start(bf16[8,144,256]{2,1,0:T(8,128)(2,1)S(1)} %panel_2_8_4_2.1), channel_id=1, source_target_pairs={{0,1},{32,35},{4,5},{36,39},{64,65},{96,99},{68,69},{100,103},{1,0... | collective-permute-start | bytes 1769480 | tf_op jit(solution)/shard_map/ppermute | solution.py:460
  86.0 1.7 %collective-permute-start.14 = (bf16[8,144,256]{2,1,0:T(8,128)(2,1)S(1)}, bf16[8,144,256]{2,1,0:T(8,128)(2,1)S(1)}, u32[]{:S(2)}, u32[]{:S(2)}) collective-permute-start(bf16[8,144,256]{2,1,0:T(8,128)(2,1)S(1)} %panel_1_8_4_2.1), channel_id=1, source_target_pairs={{0,8},{32,56},{4,12},{36,60},{64,72},{96,120},{68,76},{100,124},{1... | collective-permute-start | bytes 1769480 | tf_op jit(solution)/shard_map/ppermute | solution.py:460
  87.8 5.6 %collective-permute-done.15 = bf16[8,144,256]{2,1,0:T(8,128)(2,1)S(1)} collective-permute-done((bf16[8,144,256]{2,1,0:T(8,128)(2,1)S(1)}, bf16[8,144,256]{2,1,0:T(8,128)(2,1)S(1)}, u32[]{:S(2)}, u32[]{:S(2)}) %collective-permute-start.15) | collective-permute-done | bytes 589856 | tf_op jit(solution)/shard_map/ppermute | solution.py:460
  93.3 2.6 %collective-permute-done.14 = bf16[8,144,256]{2,1,0:T(8,128)(2,1)S(1)} collective-permute-done((bf16[8,144,256]{2,1,0:T(8,128)(2,1)S(1)}, bf16[8,144,256]{2,1,0:T(8,128)(2,1)S(1)}, u32[]{:S(2)}, u32[]{:S(2)}) %collective-permute-start.14) | collective-permute-done | bytes 589856 | tf_op jit(solution)/shard_map/ppermute | solution.py:460
  96.0 0.7 fusion.7
  96.7 0.1 fusion.8
  96.8 0.1 collective-permute-start.16
  96.9 0.1 collective-permute-start.17
  97.0 2.5 %collective-permute-start.18 = (bf16[2,448,256]{2,1,0:T(8,128)(2,1)S(1)}, bf16[2,448,256]{2,1,0:T(8,128)(2,1)S(1)}, u32[]{:S(2)}, u32[]{:S(2)}) collective-permute-start(bf16[2,448,256]{2,1,0:T(8,128)(2,1)S(1)} %get-tuple-element.110), channel_id=1, source_target_pairs={{0,3},{32,33},{4,7},{36,37},{64,67},{96,97},{68,71},{100,101},{1,2... | collective-permute-start | bytes 1376264 | tf_op jit(solution)/shard_map/ppermute | solution.py:460
  99.5 0.5 collective-permute-start.19
  100.0 2.1 %load_state.1 = (f32[224,2048]{1,0:T(8,128)S(1)}, f32[224,2048]{1,0:T(8,128)S(1)}) custom-call(f32[224,2048]{1,0:T(8,128)} %master, f32[224,2048]{1,0:T(8,128)} %moment), custom_call_target="tpu_custom_call" | custom-call | flops 1 | bytes 1 | tf_op jit(solution)/shard_map/load_state/pallas_call | solution.py:371
  102.1 6.2 %collective-permute-done.19 = bf16[112,1024]{1,0:T(8,128)(2,1)S(1)} collective-permute-done((bf16[112,1024]{1,0:T(8,128)(2,1)S(1)}, bf16[112,1024]{1,0:T(8,128)(2,1)S(1)}, u32[]{:S(2)}, u32[]{:S(2)}) %collective-permute-start.19) | collective-permute-done | bytes 229408 | tf_op jit(solution)/shard_map/ppermute | solution.py:460
  108.3 1.7 %collective-permute-done.18 = bf16[2,448,256]{2,1,0:T(8,128)(2,1)S(1)} collective-permute-done((bf16[2,448,256]{2,1,0:T(8,128)(2,1)S(1)}, bf16[2,448,256]{2,1,0:T(8,128)(2,1)S(1)}, u32[]{:S(2)}, u32[]{:S(2)}) %collective-permute-start.18) | collective-permute-done | bytes 458784 | tf_op jit(solution)/shard_map/ppermute | solution.py:460
  110.2 0.2 fusion.1
  110.5 0.3 collective-permute-start.20
  110.8 1.4 %collective-permute-start.21 = (bf16[448,256]{1,0:T(8,128)(2,1)S(1)}, bf16[448,256]{1,0:T(8,128)(2,1)S(1)}, u32[]{:S(2)}, u32[]{:S(2)}) collective-permute-start(bf16[448,256]{1,0:T(8,128)(2,1)S(1)} %fusion.5.own), channel_id=1, source_target_pairs={{0,64},{32,96},{4,68},{36,100},{64,0},{96,32},{68,4},{100,36},{1,6... | collective-permute-start | bytes 688136 | tf_op jit(solution)/shard_map/ppermute | solution.py:460
  112.2 2.2 %collective-permute-start.22 = (bf16[448,256]{1,0:T(8,128)(2,1)S(1)}, bf16[448,256]{1,0:T(8,128)(2,1)S(1)}, u32[]{:S(2)}, u32[]{:S(2)}) collective-permute-start(bf16[448,256]{1,0:T(8,128)(2,1)S(1)} %fusion.6), channel_id=1, source_target_pairs={{0,4},{32,100},{4,0},{36,96},{64,68},{96,36},{68,64},{100,32},{1,5... | collective-permute-start | bytes 688136 | tf_op jit(solution)/shard_map/ppermute | solution.py:460
  115.0 0.7 collective-permute-done.20.own_rest
  115.7 3.9 %collective-permute-done.21.far_own = bf16[448,256]{1,0:T(8,128)(2,1)S(1)} collective-permute-done((bf16[448,256]{1,0:T(8,128)(2,1)S(1)}, bf16[448,256]{1,0:T(8,128)(2,1)S(1)}, u32[]{:S(2)}, u32[]{:S(2)}) %collective-permute-start.21) | collective-permute-done | bytes 229408 | tf_op jit(solution)/shard_map/ppermute | solution.py:460
  119.6 5.1 %collective-permute-done.22.far_rest = bf16[448,256]{1,0:T(8,128)(2,1)S(1)} collective-permute-done((bf16[448,256]{1,0:T(8,128)(2,1)S(1)}, bf16[448,256]{1,0:T(8,128)(2,1)S(1)}, u32[]{:S(2)}, u32[]{:S(2)}) %collective-permute-start.22) | collective-permute-done | bytes 229408 | tf_op jit(solution)/shard_map/ppermute | solution.py:460
  124.7 0.7 combine.1.mine
  125.5 0.1 collective-permute-start.23
  125.6 1.8 %collective-permute-done.23.theirs = bf16[112,2048]{1,0:T(8,128)(2,1)S(1)} collective-permute-done((bf16[112,2048]{1,0:T(8,128)(2,1)S(1)}, bf16[112,2048]{1,0:T(8,128)(2,1)S(1)}, u32[]{:S(2)}, u32[]{:S(2)}) %collective-permute-start.23) | collective-permute-done | bytes 458784 | tf_op jit(solution)/shard_map/ppermute | solution.py:460
  127.4 2.4 %update.1 = (bf16[224,2048]{1,0:T(8,128)(2,1)}, f32[224,2048]{1,0:T(8,128)}) custom-call(s32[4]{0:T(128)S(1)} %pad_add_fusion.where, bf16[112,2048]{1,0:T(8,128)(2,1)S(1)} %combine.1.mine, bf16[112,2048]{1,0:T(8,128)(2,1)S(1)} %collective-permute-done.23.theirs, f32[224,2048]{1,0:T(8,128)S(1)} %get-tuple-element.106.master, ...), custom_call_target="tpu_custom_call" | custom-call | flops 1 | bytes 1 | tf_op jit(solution)/shard_map/update/pallas_call | solution.py:440
  (32 shorter events, 0.3 us)
Async XLA Ops:
  0.6 12.4 %collective-permute-start.2 = (bf16[896,2048]{1,0:T(8,128)(2,1)}, bf16[896,2048]{1,0:T(8,128)(2,1)}, u32[]{:S(2)}, u32[]{:S(2)}) collective-permute-start(bf16[896,2048]{1,0:T(8,128)(2,1)} %grads.1), channel_id=1, source_target_pairs={{0,32},{32,0},{4,36},{36,4},{64,96},{96,64},{68,100},{100,68},{1,3... | collective-permute-start | bytes 11010056 | tf_op jit(solution)/shard_map/ppermute | solution.py:460
  6.9 14.9 %collective-permute-start.1 = (bf16[3,32,112,128]{3,2,1,0:T(8,128)(2,1)}, bf16[3,32,112,128]{3,2,1,0:T(8,128)(2,1)S(1)}, u32[]{:S(2)}, u32[]{:S(2)}) collective-permute-start(bf16[3,32,112,128]{3,2,1,0:T(8,128)(2,1)} %get-tuple-element.59), channel_id=1, source_target_pairs={{0,32},{32,0},{4,36},{36,4},{64,96},{96,64},{68,100},{100,68},{1,3... | collective-permute-start | bytes 8257544 | tf_op jit(solution)/shard_map/ppermute | solution.py:460
  7.1 6.0 %copy-start.1 = (s32[4]{0:T(128)S(1)}, s32[4]{0:T(128)}, u32[]{:S(2)}) copy-start(s32[4]{0:T(128)} %mixture.3) | copy-start | bytes 52
  12.5 9.7 %collective-permute-start = (bf16[4,32,112,128]{3,2,1,0:T(8,128)(2,1)}, bf16[4,32,112,128]{3,2,1,0:T(8,128)(2,1)S(1)}, u32[]{:S(2)}, u32[]{:S(2)}) collective-permute-start(bf16[4,32,112,128]{3,2,1,0:T(8,128)(2,1)} %get-tuple-element.58), channel_id=1, source_target_pairs={{0,32},{32,0},{4,36},{36,4},{64,96},{96,64},{68,100},{100,68},{1,3... | collective-permute-start | bytes 11010056 | tf_op jit(solution)/shard_map/ppermute | solution.py:460
  24.8 24.2 %collective-permute-start.3 = (bf16[16,160,256]{2,1,0:T(8,128)(2,1)S(1)}, bf16[16,160,256]{2,1,0:T(8,128)(2,1)S(1)}, u32[]{:S(2)}, u32[]{:S(2)}) collective-permute-start(bf16[16,160,256]{2,1,0:T(8,128)(2,1)S(1)} %panel_0_48_2_1.1), channel_id=1, source_target_pairs={{0,8},{32,56},{4,12},{36,60},{64,72},{96,120},{68,76},{100,124},{1... | collective-permute-start | bytes 3932168 | tf_op jit(solution)/shard_map/ppermute | solution.py:460
  29.9 23.0 %collective-permute-start.4 = (bf16[16,144,256]{2,1,0:T(8,128)(2,1)S(1)}, bf16[16,144,256]{2,1,0:T(8,128)(2,1)S(1)}, u32[]{:S(2)}, u32[]{:S(2)}) collective-permute-start(bf16[16,144,256]{2,1,0:T(8,128)(2,1)S(1)} %panel_1_48_2_1.1), channel_id=1, source_target_pairs={{0,1},{32,35},{4,5},{36,39},{64,65},{96,99},{68,69},{100,103},{1,0... | collective-permute-start | bytes 3538952 | tf_op jit(solution)/shard_map/ppermute | solution.py:460
  36.7 21.9 %collective-permute-start.5 = (bf16[16,144,256]{2,1,0:T(8,128)(2,1)S(1)}, bf16[16,144,256]{2,1,0:T(8,128)(2,1)S(1)}, u32[]{:S(2)}, u32[]{:S(2)}) collective-permute-start(bf16[16,144,256]{2,1,0:T(8,128)(2,1)S(1)} %panel_2_48_4_0.1), channel_id=1, source_target_pairs={{0,4},{32,100},{4,0},{36,96},{64,68},{96,36},{68,64},{100,32},{1,5... | collective-permute-start | bytes 3538952 | tf_op jit(solution)/shard_map/ppermute | solution.py:460
  42.6 21.7 %collective-permute-start.6 = (bf16[16,160,256]{2,1,0:T(8,128)(2,1)S(1)}, bf16[16,160,256]{2,1,0:T(8,128)(2,1)S(1)}, u32[]{:S(2)}, u32[]{:S(2)}) collective-permute-start(bf16[16,160,256]{2,1,0:T(8,128)(2,1)S(1)} %panel_0_32_4_0.1), channel_id=1, source_target_pairs={{0,8},{32,56},{4,12},{36,60},{64,72},{96,120},{68,76},{100,124},{1... | collective-permute-start | bytes 3932168 | tf_op jit(solution)/shard_map/ppermute | solution.py:460
  45.8 23.2 %collective-permute-start.7 = (bf16[16,144,256]{2,1,0:T(8,128)(2,1)S(1)}, bf16[16,144,256]{2,1,0:T(8,128)(2,1)S(1)}, u32[]{:S(2)}, u32[]{:S(2)}) collective-permute-start(bf16[16,144,256]{2,1,0:T(8,128)(2,1)S(1)} %panel_1_32_4_0.1), channel_id=1, source_target_pairs={{0,1},{32,35},{4,5},{36,39},{64,65},{96,99},{68,69},{100,103},{1,0... | collective-permute-start | bytes 3538952 | tf_op jit(solution)/shard_map/ppermute | solution.py:460
  49.1 22.0 %collective-permute-start.8 = (bf16[16,144,256]{2,1,0:T(8,128)(2,1)S(1)}, bf16[16,144,256]{2,1,0:T(8,128)(2,1)S(1)}, u32[]{:S(2)}, u32[]{:S(2)}) collective-permute-start(bf16[16,144,256]{2,1,0:T(8,128)(2,1)S(1)} %panel_2_32_4_0.1), channel_id=1, source_target_pairs={{0,4},{32,100},{4,0},{36,96},{64,68},{96,36},{68,64},{100,32},{1,5... | collective-permute-start | bytes 3538952 | tf_op jit(solution)/shard_map/ppermute | solution.py:460
  52.9 23.3 %collective-permute-start.9 = (bf16[16,160,256]{2,1,0:T(8,128)(2,1)S(1)}, bf16[16,160,256]{2,1,0:T(8,128)(2,1)S(1)}, u32[]{:S(2)}, u32[]{:S(2)}) collective-permute-start(bf16[16,160,256]{2,1,0:T(8,128)(2,1)S(1)} %panel_0_16_4_1.1), channel_id=1, source_target_pairs={{0,1},{32,35},{4,5},{36,39},{64,65},{96,99},{68,69},{100,103},{1,0... | collective-permute-start | bytes 3932168 | tf_op jit(solution)/shard_map/ppermute | solution.py:460
  58.7 20.5 %collective-permute-start.10 = (bf16[16,144,256]{2,1,0:T(8,128)(2,1)S(1)}, bf16[16,144,256]{2,1,0:T(8,128)(2,1)S(1)}, u32[]{:S(2)}, u32[]{:S(2)}) collective-permute-start(bf16[16,144,256]{2,1,0:T(8,128)(2,1)S(1)} %panel_1_16_4_1.1), channel_id=1, source_target_pairs={{0,4},{32,100},{4,0},{36,96},{64,68},{96,36},{68,64},{100,32},{1,5... | collective-permute-start | bytes 3538952 | tf_op jit(solution)/shard_map/ppermute | solution.py:460
  64.3 16.9 %collective-permute-start.11 = (bf16[16,144,256]{2,1,0:T(8,128)(2,1)S(1)}, bf16[16,144,256]{2,1,0:T(8,128)(2,1)S(1)}, u32[]{:S(2)}, u32[]{:S(2)}) collective-permute-start(bf16[16,144,256]{2,1,0:T(8,128)(2,1)S(1)} %panel_2_16_4_1.1), channel_id=1, source_target_pairs={{0,8},{32,56},{4,12},{36,60},{64,72},{96,120},{68,76},{100,124},{1... | collective-permute-start | bytes 3538952 | tf_op jit(solution)/shard_map/ppermute | solution.py:460
  75.1 3.3 %collective-permute-start.13 = (bf16[112,2048]{1,0:T(8,128)(2,1)S(1)}, bf16[112,2048]{1,0:T(8,128)(2,1)S(1)}, u32[]{:S(2)}, u32[]{:S(2)}) collective-permute-start(bf16[112,2048]{1,0:T(8,128)(2,1)S(1)} %get-tuple-element.84), channel_id=1, source_target_pairs={{0,32},{32,0},{4,36},{36,4},{64,96},{96,64},{68,100},{100,68},{1,3... | collective-permute-start | bytes 1376264 | tf_op jit(solution)/shard_map/ppermute | solution.py:460
  78.2 17.8 %collective-permute-start.12 = (bf16[8,160,256]{2,1,0:T(8,128)(2,1)S(1)}, bf16[8,160,256]{2,1,0:T(8,128)(2,1)S(1)}, u32[]{:S(2)}, u32[]{:S(2)}) collective-permute-start(bf16[8,160,256]{2,1,0:T(8,128)(2,1)S(1)} %panel_0_8_4_2.1), channel_id=1, source_target_pairs={{0,4},{32,100},{4,0},{36,96},{64,68},{96,36},{68,64},{100,32},{1,5... | collective-permute-start | bytes 1966088 | tf_op jit(solution)/shard_map/ppermute | solution.py:460
  81.2 6.4 %copy-start = (bf16[16,144,256]{2,1,0:T(8,128)(2,1)}, bf16[16,144,256]{2,1,0:T(8,128)(2,1)S(1)}, u32[]{:S(2)}) copy-start(bf16[16,144,256]{2,1,0:T(8,128)(2,1)S(1)} %collective-permute-done.11.rest_5_) | copy-start | bytes 3538948
  83.3 10.0 %collective-permute-start.15 = (bf16[8,144,256]{2,1,0:T(8,128)(2,1)S(1)}, bf16[8,144,256]{2,1,0:T(8,128)(2,1)S(1)}, u32[]{:S(2)}, u32[]{:S(2)}) collective-permute-start(bf16[8,144,256]{2,1,0:T(8,128)(2,1)S(1)} %panel_2_8_4_2.1), channel_id=1, source_target_pairs={{0,1},{32,35},{4,5},{36,39},{64,65},{96,99},{68,69},{100,103},{1,0... | collective-permute-start | bytes 1769480 | tf_op jit(solution)/shard_map/ppermute | solution.py:460
  86.0 9.9 %collective-permute-start.14 = (bf16[8,144,256]{2,1,0:T(8,128)(2,1)S(1)}, bf16[8,144,256]{2,1,0:T(8,128)(2,1)S(1)}, u32[]{:S(2)}, u32[]{:S(2)}) collective-permute-start(bf16[8,144,256]{2,1,0:T(8,128)(2,1)S(1)} %panel_1_8_4_2.1), channel_id=1, source_target_pairs={{0,8},{32,56},{4,12},{36,60},{64,72},{96,120},{68,76},{100,124},{1... | collective-permute-start | bytes 1769480 | tf_op jit(solution)/shard_map/ppermute | solution.py:460
  87.7 8.3 %slice-start = ((bf16[16,144,256]{2,1,0:T(8,128)(2,1)}), bf16[8,144,256]{2,1,0:T(8,128)(2,1)S(1)}, s32[]{:S(2)}) async-start(bf16[16,144,256]{2,1,0:T(8,128)(2,1)} %copy-done), calls=%async_computation | async-start | bytes 1179648 | tf_op jit(solution)/shard_map/slice | solution.py:544
  96.8 11.5 %collective-permute-start.16 = (bf16[2,448,256]{2,1,0:T(8,128)(2,1)S(1)}, bf16[2,448,256]{2,1,0:T(8,128)(2,1)S(1)}, u32[]{:S(2)}, u32[]{:S(2)}) collective-permute-start(bf16[2,448,256]{2,1,0:T(8,128)(2,1)S(1)} %get-tuple-element.112), channel_id=1, source_target_pairs={{0,27},{32,41},{4,31},{36,45},{64,91},{96,105},{68,95},{100,109},{... | collective-permute-start | bytes 1376264 | tf_op jit(solution)/shard_map/ppermute | solution.py:460
  96.9 11.4 %collective-permute-start.17 = (bf16[2,448,256]{2,1,0:T(8,128)(2,1)S(1)}, bf16[2,448,256]{2,1,0:T(8,128)(2,1)S(1)}, u32[]{:S(2)}, u32[]{:S(2)}) collective-permute-start(bf16[2,448,256]{2,1,0:T(8,128)(2,1)S(1)} %get-tuple-element.111), channel_id=1, source_target_pairs={{0,24},{32,40},{4,28},{36,44},{64,88},{96,104},{68,92},{100,108},{... | collective-permute-start | bytes 1376264 | tf_op jit(solution)/shard_map/ppermute | solution.py:460
  97.0 13.0 %collective-permute-start.18 = (bf16[2,448,256]{2,1,0:T(8,128)(2,1)S(1)}, bf16[2,448,256]{2,1,0:T(8,128)(2,1)S(1)}, u32[]{:S(2)}, u32[]{:S(2)}) collective-permute-start(bf16[2,448,256]{2,1,0:T(8,128)(2,1)S(1)} %get-tuple-element.110), channel_id=1, source_target_pairs={{0,3},{32,33},{4,7},{36,37},{64,67},{96,97},{68,71},{100,101},{1,2... | collective-permute-start | bytes 1376264 | tf_op jit(solution)/shard_map/ppermute | solution.py:460
  99.5 8.8 %collective-permute-start.19 = (bf16[112,1024]{1,0:T(8,128)(2,1)S(1)}, bf16[112,1024]{1,0:T(8,128)(2,1)S(1)}, u32[]{:S(2)}, u32[]{:S(2)}) collective-permute-start(bf16[112,1024]{1,0:T(8,128)(2,1)S(1)} %get-tuple-element.92), channel_id=1, source_target_pairs={{0,64},{32,96},{4,68},{36,100},{64,0},{96,32},{68,4},{100,36},{1,6... | collective-permute-start | bytes 688136 | tf_op jit(solution)/shard_map/ppermute | solution.py:460
  110.5 5.2 %collective-permute-start.20 = (bf16[448,256]{1,0:T(8,128)(2,1)S(1)}, bf16[448,256]{1,0:T(8,128)(2,1)S(1)}, u32[]{:S(2)}, u32[]{:S(2)}) collective-permute-start(bf16[448,256]{1,0:T(8,128)(2,1)S(1)} %fusion.6), channel_id=1, source_target_pairs={{0,68},{32,36},{4,64},{36,32},{64,4},{96,100},{68,0},{100,96},{1,6... | collective-permute-start | bytes 688136 | tf_op jit(solution)/shard_map/ppermute | solution.py:460
  110.8 8.8 %collective-permute-start.21 = (bf16[448,256]{1,0:T(8,128)(2,1)S(1)}, bf16[448,256]{1,0:T(8,128)(2,1)S(1)}, u32[]{:S(2)}, u32[]{:S(2)}) collective-permute-start(bf16[448,256]{1,0:T(8,128)(2,1)S(1)} %fusion.5.own), channel_id=1, source_target_pairs={{0,64},{32,96},{4,68},{36,100},{64,0},{96,32},{68,4},{100,36},{1,6... | collective-permute-start | bytes 688136 | tf_op jit(solution)/shard_map/ppermute | solution.py:460
  112.2 12.5 %collective-permute-start.22 = (bf16[448,256]{1,0:T(8,128)(2,1)S(1)}, bf16[448,256]{1,0:T(8,128)(2,1)S(1)}, u32[]{:S(2)}, u32[]{:S(2)}) collective-permute-start(bf16[448,256]{1,0:T(8,128)(2,1)S(1)} %fusion.6), channel_id=1, source_target_pairs={{0,4},{32,100},{4,0},{36,96},{64,68},{96,36},{68,64},{100,32},{1,5... | collective-permute-start | bytes 688136 | tf_op jit(solution)/shard_map/ppermute | solution.py:460
  125.5 1.9 %collective-permute-start.23 = (bf16[112,2048]{1,0:T(8,128)(2,1)S(1)}, bf16[112,2048]{1,0:T(8,128)(2,1)S(1)}, u32[]{:S(2)}, u32[]{:S(2)}) collective-permute-start(bf16[112,2048]{1,0:T(8,128)(2,1)S(1)} %combine.1.mine), channel_id=1, source_target_pairs={{0,32},{32,0},{4,36},{36,4},{64,96},{96,64},{68,100},{100,68},{1,3... | collective-permute-start | bytes 1376264 | tf_op jit(solution)/shard_map/ppermute | solution.py:460
where the time goes:
time: 130 us
  Pallas kernels  66 us (51%)
  starting transfers between devices  32.1 us (25%)
  waiting for transfers between devices  28.6 us (22%)
  between operations  1.88 us (1%)
    pallas_call x17, Pallas kernels, panel(): pl.pallas_call(functools.partial(panel_kernel, first, part, tuple((offset...  43 us
    ppermute x24, starting transfers between devices, send(): return lax.ppermute(value, AXES, pairs)  32.1 us
    ppermute x24, waiting for transfers between devices, send(): return lax.ppermute(value, AXES, pairs)  28.6 us
    pallas_call x2, Pallas kernels, transposed(): pl.pallas_call(functools.partial(transpose_kernel, begin), in_specs=[pl.B...  10.1 us
    pallas_call x1, Pallas kernels, scaled(): pl.pallas_call(scale_kernel, in_specs=[pl.BlockSpec(memory_space=pltpu.SM...  4.33 us
  transfers between devices with their start and end apart: 24, of which 9 were waited for; matrix products, arithmetic and copies ran while one was open for 0% of the time, Pallas kernels for 46%

commit v1 on v0

--- a/solution.py
+++ b/solution.py
@@ -354,6 +354,27 @@
         cost_estimate=MODEST,
         name=f"panel_{part}_{first}_{len(operands)}_{len(received)}",
     )(where, *[in_vmem(v) for v in operands], *[v for v, _ in received])
+
+
+def message_kernel(local, received, out):
+    count = out.shape[0]
+
+    @pl.loop(0, count)
+    def _(k):
+        total = local[count + k].astype(jnp.float32) + received[count + k].astype(jnp.float32)
+        out[k] = total.astype(out.dtype)
+
+
+def message(local, received, part):
+    return pl.pallas_call(
+        message_kernel,
+        in_specs=[pl.BlockSpec(memory_space=pltpu.VMEM)] * 2,
+        out_specs=pl.BlockSpec(memory_space=pltpu.VMEM),
+        out_shape=jax.ShapeDtypeStruct((local.shape[0] // 2, *local.shape[1:]), local.dtype),
+        compiler_params=pltpu.CompilerParams(vmem_limit_bytes=6 << 20),
+        cost_estimate=QUICK,
+        name=f"message_{part}",
+    )(local, received)
 
 
 def load_state_kernel(master, moment, master_out, moment_out, sems):
@@ -524,18 +545,15 @@
     got_far = step(0, far)
     got_near = step(0, chunk(32, 16, [()] * PARTS))
     got = step(1, chunk(16, 16, [((v, 0),) for v in got_far]))
-    local = chunk(0, 8, [((v, 0),) for v in got_near])
+    local = chunk(0, 16, [((v, 0),) for v in got_near])
 
     mine, theirs = weighted_drift(where, mixture, after(island_drift, *last))
     drift_near = send(theirs, swap)
-    last = [mine]
-    out = []
+    out = [mine]
     for p in range(PARTS):
-        out.append(product(operands, p, 8, 8, ((got_near[p], 8), (got[p], 8))))
-        if p == 0:
-            mine, theirs = added_drift(where, after(mine, *last), drift_near)
-            last = [mine]
-    third = step(2, out)
+        out.append(message(after(local[p], out[-1]), got[p], p))
+    third = step(2, out[1:])
+    mine, theirs = added_drift(where, after(mine, out[-1]), drift_near)
     rows = mine.shape[0]
     *third, theirs = lax.optimization_barrier((*third, theirs))
     drift_far = send(theirs, permutation(opposite))

time: 130 us -> 125 us (0.962)
  Pallas kernels: 66 us -> 64 us
  starting transfers between devices: 32.1 us -> 30.2 us
  waiting for transfers between devices: 28.6 us -> 27.3 us
    pallas_call x17 -> x14, Pallas kernels: 43 us -> 40.5 us  [panel(): pl.pallas_call(functools.partial(panel_kernel, first, part, tuple((offset...]
    ppermute x24, starting transfers between devices: 32.1 us -> 30.2 us  [send(): return lax.ppermute(value, AXES, pairs)]
  transfers between devices with their start and end apart: 24 -> 24, of which waited for: 9 -> 10; matrix products, arithmetic and copies ran while one was open for 0% -> 0% of each run, Pallas kernels for 46% -> 47%
where the time goes in v1:
time: 125 us
  Pallas kernels  64 us (51%)
  starting transfers between devices  30.2 us (24%)
  waiting for transfers between devices  27.3 us (22%)
  between operations  1.98 us (2%)
    pallas_call x14, Pallas kernels, panel(): pl.pallas_call(functools.partial(panel_kernel, first, part, tuple((offset...  40.5 us
    ppermute x24, starting transfers between devices, send(): return lax.ppermute(value, AXES, pairs)  30.2 us
    ppermute x24, waiting for transfers between devices, send(): return lax.ppermute(value, AXES, pairs)  27.3 us
    pallas_call x2, Pallas kernels, transposed(): pl.pallas_call(functools.partial(transpose_kernel, begin), in_specs=[pl.B...  10.2 us
    pallas_call x1, Pallas kernels, scaled(): pl.pallas_call(scale_kernel, in_specs=[pl.BlockSpec(memory_space=pltpu.SM...  4.33 us
  transfers between devices with their start and end apart: 24, of which 10 were waited for; matrix products, arithmetic and copies ran while one was open for 0% of the time, Pallas kernels for 47%

profile of v1, /device:TPU:1, one launch (start us, length us, event | category | flops | bytes accessed | tf_op | source)
XLA Modules:
  0.0 125.0 jit_solution(2670617946679037973)
XLA Ops:
  0.6 1.5 %collective-permute-start.2 = (bf16[896,2048]{1,0:T(8,128)(2,1)}, bf16[896,2048]{1,0:T(8,128)(2,1)}, u32[]{:S(2)}, u32[]{:S(2)}) collective-permute-start(bf16[896,2048]{1,0:T(8,128)(2,1)} %grads.1), channel_id=1, source_target_pairs={{0,32},{32,0},{4,36},{36,4},{64,96},{96,64},{68,100},{100,68},{1,3... | collective-permute-start | bytes 11010056 | tf_op jit(solution)/shard_map/ppermute | solution.py:481
  2.1 0.1 pad_add_fusion.where
  2.2 4.7 %transpose_acts_0.1 = (bf16[2,7,32,112,128]{4,3,2,1,0:T(8,128)(2,1)S(1)}, bf16[3,32,112,128]{3,2,1,0:T(8,128)(2,1)}) custom-call(s32[4]{0:T(128)S(1)} %pad_add_fusion.where, bf16[896,7168]{1,0:T(8,128)(2,1)} %acts.3), custom_call_target="tpu_custom_call" | custom-call | flops 12000000000 | bytes 1 | tf_op jit(solution)/shard_map/transpose_acts_0/pallas_call | solution.py:136
  6.9 0.2 collective-permute-start.1
  7.1 5.5 %transpose_acts_1.1 = (bf16[2,7,32,112,128]{4,3,2,1,0:T(8,128)(2,1)S(1)}, bf16[4,32,112,128]{3,2,1,0:T(8,128)(2,1)}) custom-call(s32[4]{0:T(128)S(1)} %pad_add_fusion.where, bf16[896,7168]{1,0:T(8,128)(2,1)} %acts.3, bf16[2,7,32,112,128]{4,3,2,1,0:T(8,128)(2,1)S(1)} %get-tuple-element.55.rest_0_), custom_call_target="tpu_custom_call", output_to_operand_aliasing={{0}: (2, {})} | custom-call | flops 12000000000 | bytes 1 | tf_op jit(solution)/shard_map/transpose_acts_1/pallas_call | solution.py:136
  12.6 0.5 collective-permute-start
  13.1 4.3 %scale_grads.1 = (bf16[896,2048]{1,0:T(8,128)(2,1)S(1)}, bf16[896,2048]{1,0:T(8,128)(2,1)S(1)}) custom-call(s32[4]{0:T(128)S(1)} %pad_add_fusion.where, s32[4]{0:T(128)S(1)} %copy-done.5, bf16[896,2048]{1,0:T(8,128)(2,1)} %grads.1, bf16[896,2048]{1,0:T(8,128)(2,1)} %collective-permute-done.2.other), custom_call_target="tpu_custom_call" | custom-call | flops 99999997952 | bytes 1 | tf_op jit(solution)/shard_map/scale_grads/pallas_call | solution.py:174
  17.4 2.3 %panel_0_48_2_0.1.rest_2_ = f32[16,160,256]{2,1,0:T(8,128)S(1)} custom-call(s32[4]{0:T(128)S(1)} %pad_add_fusion.where, bf16[2,7,32,112,128]{4,3,2,1,0:T(8,128)(2,1)S(1)} %get-tuple-element.62.rest_0_, bf16[896,2048]{1,0:T(8,128)(2,1)S(1)} %get-tuple-element.60.rest_1_.rest_2_), custom_call_target="tpu_custom_call" | custom-call | flops 2000000000 | bytes 1 | tf_op jit(solution)/shard_map/panel_0_48_2_0/pallas_call | solution.py:347
  19.7 2.2 %panel_1_48_2_0.1.rest_2_ = f32[16,144,256]{2,1,0:T(8,128)S(1)} custom-call(s32[4]{0:T(128)S(1)} %pad_add_fusion.where, bf16[2,7,32,112,128]{4,3,2,1,0:T(8,128)(2,1)S(1)} %get-tuple-element.62.rest_0_, bf16[896,2048]{1,0:T(8,128)(2,1)S(1)} %get-tuple-element.60.rest_1_.rest_2_), custom_call_target="tpu_custom_call" | custom-call | flops 2000000000 | bytes 1 | tf_op jit(solution)/shard_map/panel_1_48_2_0/pallas_call | solution.py:347
  21.9 0.4 load_acts_0.1.rest_0_
  22.3 0.3 load_acts_1.1.rest_0_.rest_1_
  22.5 2.3 %panel_0_48_2_1.1 = bf16[16,160,256]{2,1,0:T(8,128)(2,1)S(1)} custom-call(s32[4]{0:T(128)S(1)} %pad_add_fusion.where, bf16[7,32,112,128]{3,2,1,0:T(8,128)(2,1)S(1)} %load_acts_1.1.rest_0_.rest_1_, bf16[896,2048]{1,0:T(8,128)(2,1)S(1)} %get-tuple-element.68.rest_1_.rest_3_, f32[16,160,256]{2,1,0:T(8,128)S(1)} %panel_0_48_2_0.1.rest_2_), custom_call_target="tpu_custom_call" | custom-call | flops 2000000000 | bytes 1 | tf_op jit(solution)/shard_map/panel_0_48_2_1/pallas_call | solution.py:347
  24.9 2.9 %collective-permute-start.3 = (bf16[16,160,256]{2,1,0:T(8,128)(2,1)S(1)}, bf16[16,160,256]{2,1,0:T(8,128)(2,1)S(1)}, u32[]{:S(2)}, u32[]{:S(2)}) collective-permute-start(bf16[16,160,256]{2,1,0:T(8,128)(2,1)S(1)} %panel_0_48_2_1.1), channel_id=1, source_target_pairs={{0,8},{32,56},{4,12},{36,60},{64,72},{96,120},{68,76},{100,124},{1... | collective-permute-start | bytes 3932168 | tf_op jit(solution)/shard_map/ppermute | solution.py:481
  27.7 2.2 %panel_1_48_2_1.1 = bf16[16,144,256]{2,1,0:T(8,128)(2,1)S(1)} custom-call(s32[4]{0:T(128)S(1)} %pad_add_fusion.where, bf16[7,32,112,128]{3,2,1,0:T(8,128)(2,1)S(1)} %load_acts_1.1.rest_0_.rest_1_, bf16[896,2048]{1,0:T(8,128)(2,1)S(1)} %get-tuple-element.68.rest_1_.rest_3_, f32[16,144,256]{2,1,0:T(8,128)S(1)} %panel_1_48_2_0.1.rest_2_), custom_call_target="tpu_custom_call" | custom-call | flops 2000000000 | bytes 1 | tf_op jit(solution)/shard_map/panel_1_48_2_1/pallas_call | solution.py:347
  29.9 3.8 %collective-permute-start.4 = (bf16[16,144,256]{2,1,0:T(8,128)(2,1)S(1)}, bf16[16,144,256]{2,1,0:T(8,128)(2,1)S(1)}, u32[]{:S(2)}, u32[]{:S(2)}) collective-permute-start(bf16[16,144,256]{2,1,0:T(8,128)(2,1)S(1)} %panel_1_48_2_1.1), channel_id=1, source_target_pairs={{0,1},{32,35},{4,5},{36,39},{64,65},{96,99},{68,69},{100,103},{1,0... | collective-permute-start | bytes 3538952 | tf_op jit(solution)/shard_map/ppermute | solution.py:481
  33.7 3.1 %panel_2_48_4_0.1 = bf16[16,144,256]{2,1,0:T(8,128)(2,1)S(1)} custom-call(s32[4]{0:T(128)S(1)} %pad_add_fusion.where, bf16[2,7,32,112,128]{4,3,2,1,0:T(8,128)(2,1)S(1)} %get-tuple-element.62.rest_0_, bf16[7,32,112,128]{3,2,1,0:T(8,128)(2,1)S(1)} %load_acts_1.1.rest_0_.rest_1_, bf16[896,2048]{1,0:T(8,128)(2,1)S(1)} %get-tuple-element.60.rest_1_.rest_2_, ...), custom_call_target="tpu_custom_call" | custom-call | flops 2000000000 | bytes 1 | tf_op jit(solution)/shard_map/panel_2_48_4_0/pallas_call | solution.py:347
  36.8 2.6 %collective-permute-start.5 = (bf16[16,144,256]{2,1,0:T(8,128)(2,1)S(1)}, bf16[16,144,256]{2,1,0:T(8,128)(2,1)S(1)}, u32[]{:S(2)}, u32[]{:S(2)}) collective-permute-start(bf16[16,144,256]{2,1,0:T(8,128)(2,1)S(1)} %panel_2_48_4_0.1), channel_id=1, source_target_pairs={{0,4},{32,100},{4,0},{36,96},{64,68},{96,36},{68,64},{100,32},{1,5... | collective-permute-start | bytes 3538952 | tf_op jit(solution)/shard_map/ppermute | solution.py:481
  39.4 3.3 %panel_0_32_4_0.1 = bf16[16,160,256]{2,1,0:T(8,128)(2,1)S(1)} custom-call(s32[4]{0:T(128)S(1)} %pad_add_fusion.where, bf16[2,7,32,112,128]{4,3,2,1,0:T(8,128)(2,1)S(1)} %get-tuple-element.62.rest_0_, bf16[7,32,112,128]{3,2,1,0:T(8,128)(2,1)S(1)} %load_acts_1.1.rest_0_.rest_1_, bf16[896,2048]{1,0:T(8,128)(2,1)S(1)} %get-tuple-element.60.rest_1_.rest_2_, ...), custom_call_target="tpu_custom_call" | custom-call | flops 2000000000 | bytes 1 | tf_op jit(solution)/shard_map/panel_0_32_4_0/pallas_call | solution.py:347
  42.7 0.1 collective-permute-start.6
  42.8 3.1 %panel_1_32_4_0.1 = bf16[16,144,256]{2,1,0:T(8,128)(2,1)S(1)} custom-call(s32[4]{0:T(128)S(1)} %pad_add_fusion.where, bf16[2,7,32,112,128]{4,3,2,1,0:T(8,128)(2,1)S(1)} %get-tuple-element.62.rest_0_, bf16[7,32,112,128]{3,2,1,0:T(8,128)(2,1)S(1)} %load_acts_1.1.rest_0_.rest_1_, bf16[896,2048]{1,0:T(8,128)(2,1)S(1)} %get-tuple-element.60.rest_1_.rest_2_, ...), custom_call_target="tpu_custom_call" | custom-call | flops 2000000000 | bytes 1 | tf_op jit(solution)/shard_map/panel_1_32_4_0/pallas_call | solution.py:347
  45.9 0.2 collective-permute-start.7
  46.0 3.1 %panel_2_32_4_0.1 = bf16[16,144,256]{2,1,0:T(8,128)(2,1)S(1)} custom-call(s32[4]{0:T(128)S(1)} %pad_add_fusion.where, bf16[2,7,32,112,128]{4,3,2,1,0:T(8,128)(2,1)S(1)} %get-tuple-element.62.rest_0_, bf16[7,32,112,128]{3,2,1,0:T(8,128)(2,1)S(1)} %load_acts_1.1.rest_0_.rest_1_, bf16[896,2048]{1,0:T(8,128)(2,1)S(1)} %get-tuple-element.60.rest_1_.rest_2_, ...), custom_call_target="tpu_custom_call" | custom-call | flops 2000000000 | bytes 1 | tf_op jit(solution)/shard_map/panel_2_32_4_0/pallas_call | solution.py:347
  49.1 0.5 collective-permute-start.8
  49.6 3.4 %panel_0_16_4_1.1 = bf16[16,160,256]{2,1,0:T(8,128)(2,1)S(1)} custom-call(s32[4]{0:T(128)S(1)} %pad_add_fusion.where, bf16[2,7,32,112,128]{4,3,2,1,0:T(8,128)(2,1)S(1)} %get-tuple-element.62.rest_0_, bf16[7,32,112,128]{3,2,1,0:T(8,128)(2,1)S(1)} %load_acts_1.1.rest_0_.rest_1_, bf16[896,2048]{1,0:T(8,128)(2,1)S(1)} %get-tuple-element.60.rest_1_.rest_2_, ...), custom_call_target="tpu_custom_call" | custom-call | flops 2000000000 | bytes 1 | tf_op jit(solution)/shard_map/panel_0_16_4_1/pallas_call | solution.py:347
  53.0 2.6 %collective-permute-start.9 = (bf16[16,160,256]{2,1,0:T(8,128)(2,1)S(1)}, bf16[16,160,256]{2,1,0:T(8,128)(2,1)S(1)}, u32[]{:S(2)}, u32[]{:S(2)}) collective-permute-start(bf16[16,160,256]{2,1,0:T(8,128)(2,1)S(1)} %panel_0_16_4_1.1), channel_id=1, source_target_pairs={{0,1},{32,35},{4,5},{36,39},{64,65},{96,99},{68,69},{100,103},{1,0... | collective-permute-start | bytes 3932168 | tf_op jit(solution)/shard_map/ppermute | solution.py:481
  55.6 3.1 %panel_1_16_4_1.1 = bf16[16,144,256]{2,1,0:T(8,128)(2,1)S(1)} custom-call(s32[4]{0:T(128)S(1)} %pad_add_fusion.where, bf16[2,7,32,112,128]{4,3,2,1,0:T(8,128)(2,1)S(1)} %get-tuple-element.62.rest_0_, bf16[7,32,112,128]{3,2,1,0:T(8,128)(2,1)S(1)} %load_acts_1.1.rest_0_.rest_1_, bf16[896,2048]{1,0:T(8,128)(2,1)S(1)} %get-tuple-element.60.rest_1_.rest_2_, ...), custom_call_target="tpu_custom_call" | custom-call | flops 2000000000 | bytes 1 | tf_op jit(solution)/shard_map/panel_1_16_4_1/pallas_call | solution.py:347
  58.7 2.6 %collective-permute-start.10 = (bf16[16,144,256]{2,1,0:T(8,128)(2,1)S(1)}, bf16[16,144,256]{2,1,0:T(8,128)(2,1)S(1)}, u32[]{:S(2)}, u32[]{:S(2)}) collective-permute-start(bf16[16,144,256]{2,1,0:T(8,128)(2,1)S(1)} %panel_1_16_4_1.1), channel_id=1, source_target_pairs={{0,4},{32,100},{4,0},{36,96},{64,68},{96,36},{68,64},{100,32},{1,5... | collective-permute-start | bytes 3538952 | tf_op jit(solution)/shard_map/ppermute | solution.py:481
  61.3 3.1 %panel_2_16_4_1.1 = bf16[16,144,256]{2,1,0:T(8,128)(2,1)S(1)} custom-call(s32[4]{0:T(128)S(1)} %pad_add_fusion.where, bf16[2,7,32,112,128]{4,3,2,1,0:T(8,128)(2,1)S(1)} %get-tuple-element.62.rest_0_, bf16[7,32,112,128]{3,2,1,0:T(8,128)(2,1)S(1)} %load_acts_1.1.rest_0_.rest_1_, bf16[896,2048]{1,0:T(8,128)(2,1)S(1)} %get-tuple-element.60.rest_1_.rest_2_, ...), custom_call_target="tpu_custom_call" | custom-call | flops 2000000000 | bytes 1 | tf_op jit(solution)/shard_map/panel_2_16_4_1/pallas_call | solution.py:347
  64.4 2.7 %collective-permute-start.11 = (bf16[16,144,256]{2,1,0:T(8,128)(2,1)S(1)}, bf16[16,144,256]{2,1,0:T(8,128)(2,1)S(1)}, u32[]{:S(2)}, u32[]{:S(2)}) collective-permute-start(bf16[16,144,256]{2,1,0:T(8,128)(2,1)S(1)} %panel_2_16_4_1.1), channel_id=1, source_target_pairs={{0,8},{32,56},{4,12},{36,60},{64,72},{96,120},{68,76},{100,124},{1... | collective-permute-start | bytes 3538952 | tf_op jit(solution)/shard_map/ppermute | solution.py:481
  67.1 3.3 %panel_0_0_4_1.1.local = bf16[16,160,256]{2,1,0:T(8,128)(2,1)S(1)} custom-call(s32[4]{0:T(128)S(1)} %pad_add_fusion.where, bf16[2,7,32,112,128]{4,3,2,1,0:T(8,128)(2,1)S(1)} %get-tuple-element.62.rest_0_, bf16[7,32,112,128]{3,2,1,0:T(8,128)(2,1)S(1)} %load_acts_1.1.rest_0_.rest_1_, bf16[896,2048]{1,0:T(8,128)(2,1)S(1)} %get-tuple-element.60.rest_1_.rest_2_, ...), custom_call_target="tpu_custom_call" | custom-call | flops 2000000000 | bytes 1 | tf_op jit(solution)/shard_map/panel_0_0_4_1/pallas_call | solution.py:347
  70.5 3.1 %panel_1_0_4_1.1.local = bf16[16,144,256]{2,1,0:T(8,128)(2,1)S(1)} custom-call(s32[4]{0:T(128)S(1)} %pad_add_fusion.where, bf16[2,7,32,112,128]{4,3,2,1,0:T(8,128)(2,1)S(1)} %get-tuple-element.62.rest_0_, bf16[7,32,112,128]{3,2,1,0:T(8,128)(2,1)S(1)} %load_acts_1.1.rest_0_.rest_1_, bf16[896,2048]{1,0:T(8,128)(2,1)S(1)} %get-tuple-element.60.rest_1_.rest_2_, ...), custom_call_target="tpu_custom_call" | custom-call | flops 2000000000 | bytes 1 | tf_op jit(solution)/shard_map/panel_1_0_4_1/pallas_call | solution.py:347
  73.6 3.1 %panel_2_0_4_1.1.local = bf16[16,144,256]{2,1,0:T(8,128)(2,1)S(1)} custom-call(s32[4]{0:T(128)S(1)} %pad_add_fusion.where, bf16[2,7,32,112,128]{4,3,2,1,0:T(8,128)(2,1)S(1)} %get-tuple-element.62.rest_0_, bf16[7,32,112,128]{3,2,1,0:T(8,128)(2,1)S(1)} %load_acts_1.1.rest_0_.rest_1_, bf16[896,2048]{1,0:T(8,128)(2,1)S(1)} %get-tuple-element.60.rest_1_.rest_2_, ...), custom_call_target="tpu_custom_call" | custom-call | flops 2000000000 | bytes 1 | tf_op jit(solution)/shard_map/panel_2_0_4_1/pallas_call | solution.py:347
  76.7 2.1 %weigh_drift.1 = (f32[112,2048]{1,0:T(8,128)S(1)}, bf16[112,2048]{1,0:T(8,128)(2,1)S(1)}) custom-call(s32[4]{0:T(128)S(1)} %pad_add_fusion.where, s32[4]{0:T(128)S(1)} %copy-done.5, f32[1,224,2048]{2,1,0:T(8,128)} %drift), custom_call_target="tpu_custom_call" | custom-call | flops 1 | bytes 1 | tf_op jit(solution)/shard_map/weigh_drift/pallas_call | solution.py:226
  78.8 0.2 message_0.1
  79.0 0.3 collective-permute-start.12
  79.2 0.2 message_1.1
  79.4 1.3 %collective-permute-done.11.received = bf16[16,144,256]{2,1,0:T(8,128)(2,1)S(1)} collective-permute-done((bf16[16,144,256]{2,1,0:T(8,128)(2,1)S(1)}, bf16[16,144,256]{2,1,0:T(8,128)(2,1)S(1)}, u32[]{:S(2)}, u32[]{:S(2)}) %collective-permute-start.11) | collective-permute-done | bytes 1179680 | tf_op jit(solution)/shard_map/ppermute | solution.py:481
  80.7 0.2 message_2.1
  80.9 0.4 collective-permute-start.14
  81.3 2.7 %collective-permute-start.13 = (bf16[8,144,256]{2,1,0:T(8,128)(2,1)S(1)}, bf16[8,144,256]{2,1,0:T(8,128)(2,1)S(1)}, u32[]{:S(2)}, u32[]{:S(2)}) collective-permute-start(bf16[8,144,256]{2,1,0:T(8,128)(2,1)S(1)} %message_1.1), channel_id=1, source_target_pairs={{0,8},{32,56},{4,12},{36,60},{64,72},{96,120},{68,76},{100,124},{1... | collective-permute-start | bytes 1769480 | tf_op jit(solution)/shard_map/ppermute | solution.py:481
  84.1 1.7 %collective-permute-done.15.received = bf16[112,2048]{1,0:T(8,128)(2,1)S(1)} collective-permute-done((bf16[112,2048]{1,0:T(8,128)(2,1)S(1)}, bf16[112,2048]{1,0:T(8,128)(2,1)S(1)}, u32[]{:S(2)}, u32[]{:S(2)}) %collective-permute-start.15) | collective-permute-done | bytes 458784 | tf_op jit(solution)/shard_map/ppermute | solution.py:481
  85.8 0.7 add_drift.1
  86.5 4.4 %collective-permute-done.14 = bf16[8,144,256]{2,1,0:T(8,128)(2,1)S(1)} collective-permute-done((bf16[8,144,256]{2,1,0:T(8,128)(2,1)S(1)}, bf16[8,144,256]{2,1,0:T(8,128)(2,1)S(1)}, u32[]{:S(2)}, u32[]{:S(2)}) %collective-permute-start.14) | collective-permute-done | bytes 589856 | tf_op jit(solution)/shard_map/ppermute | solution.py:481
  90.9 0.4 collective-permute-done.13
  91.3 0.8 fusion.7
  92.1 0.1 fusion.8
  92.2 0.1 collective-permute-start.16
  92.3 0.1 collective-permute-start.17
  92.4 2.5 %collective-permute-start.18 = (bf16[2,448,256]{2,1,0:T(8,128)(2,1)S(1)}, bf16[2,448,256]{2,1,0:T(8,128)(2,1)S(1)}, u32[]{:S(2)}, u32[]{:S(2)}) collective-permute-start(bf16[2,448,256]{2,1,0:T(8,128)(2,1)S(1)} %get-tuple-element.110), channel_id=1, source_target_pairs={{0,3},{32,33},{4,7},{36,37},{64,67},{96,97},{68,71},{100,101},{1,2... | collective-permute-start | bytes 1376264 | tf_op jit(solution)/shard_map/ppermute | solution.py:481
  95.0 2.1 %load_state.1 = (f32[224,2048]{1,0:T(8,128)S(1)}, f32[224,2048]{1,0:T(8,128)S(1)}) custom-call(f32[224,2048]{1,0:T(8,128)} %master, f32[224,2048]{1,0:T(8,128)} %moment), custom_call_target="tpu_custom_call" | custom-call | flops 1 | bytes 1 | tf_op jit(solution)/shard_map/load_state/pallas_call | solution.py:392
  97.0 6.8 %collective-permute-done.19 = bf16[112,1024]{1,0:T(8,128)(2,1)S(1)} collective-permute-done((bf16[112,1024]{1,0:T(8,128)(2,1)S(1)}, bf16[112,1024]{1,0:T(8,128)(2,1)S(1)}, u32[]{:S(2)}, u32[]{:S(2)}) %collective-permute-start.19) | collective-permute-done | bytes 229408 | tf_op jit(solution)/shard_map/ppermute | solution.py:481
  103.8 1.7 %collective-permute-done.18 = bf16[2,448,256]{2,1,0:T(8,128)(2,1)S(1)} collective-permute-done((bf16[2,448,256]{2,1,0:T(8,128)(2,1)S(1)}, bf16[2,448,256]{2,1,0:T(8,128)(2,1)S(1)}, u32[]{:S(2)}, u32[]{:S(2)}) %collective-permute-start.18) | collective-permute-done | bytes 458784 | tf_op jit(solution)/shard_map/ppermute | solution.py:481
  105.6 0.2 fusion.1
  105.9 0.1 fusion.5.own
  105.9 0.1 collective-permute-start.20
  106.0 2.5 %collective-permute-start.21 = (bf16[448,256]{1,0:T(8,128)(2,1)S(1)}, bf16[448,256]{1,0:T(8,128)(2,1)S(1)}, u32[]{:S(2)}, u32[]{:S(2)}) collective-permute-start(bf16[448,256]{1,0:T(8,128)(2,1)S(1)} %fusion.5.own), channel_id=1, source_target_pairs={{0,64},{32,96},{4,68},{36,100},{64,0},{96,32},{68,4},{100,36},{1,6... | collective-permute-start | bytes 688136 | tf_op jit(solution)/shard_map/ppermute | solution.py:481
  108.5 1.4 %collective-permute-start.22 = (bf16[448,256]{1,0:T(8,128)(2,1)S(1)}, bf16[448,256]{1,0:T(8,128)(2,1)S(1)}, u32[]{:S(2)}, u32[]{:S(2)}) collective-permute-start(bf16[448,256]{1,0:T(8,128)(2,1)S(1)} %fusion.6), channel_id=1, source_target_pairs={{0,4},{32,100},{4,0},{36,96},{64,68},{96,36},{68,64},{100,32},{1,5... | collective-permute-start | bytes 688136 | tf_op jit(solution)/shard_map/ppermute | solution.py:481
  110.5 0.7 collective-permute-done.20.own_rest
  111.2 5.1 %collective-permute-done.21.far_own = bf16[448,256]{1,0:T(8,128)(2,1)S(1)} collective-permute-done((bf16[448,256]{1,0:T(8,128)(2,1)S(1)}, bf16[448,256]{1,0:T(8,128)(2,1)S(1)}, u32[]{:S(2)}, u32[]{:S(2)}) %collective-permute-start.21) | collective-permute-done | bytes 229408 | tf_op jit(solution)/shard_map/ppermute | solution.py:481
  116.2 3.6 %collective-permute-done.22.far_rest = bf16[448,256]{1,0:T(8,128)(2,1)S(1)} collective-permute-done((bf16[448,256]{1,0:T(8,128)(2,1)S(1)}, bf16[448,256]{1,0:T(8,128)(2,1)S(1)}, u32[]{:S(2)}, u32[]{:S(2)}) %collective-permute-start.22) | collective-permute-done | bytes 229408 | tf_op jit(solution)/shard_map/ppermute | solution.py:481
  119.8 0.7 combine.1.mine
  120.5 0.1 collective-permute-start.23
  120.6 1.8 %collective-permute-done.23.theirs = bf16[112,2048]{1,0:T(8,128)(2,1)S(1)} collective-permute-done((bf16[112,2048]{1,0:T(8,128)(2,1)S(1)}, bf16[112,2048]{1,0:T(8,128)(2,1)S(1)}, u32[]{:S(2)}, u32[]{:S(2)}) %collective-permute-start.23) | collective-permute-done | bytes 458784 | tf_op jit(solution)/shard_map/ppermute | solution.py:481
  122.4 2.4 %update.1 = (bf16[224,2048]{1,0:T(8,128)(2,1)}, f32[224,2048]{1,0:T(8,128)}) custom-call(s32[4]{0:T(128)S(1)} %pad_add_fusion.where, bf16[112,2048]{1,0:T(8,128)(2,1)S(1)} %combine.1.mine, bf16[112,2048]{1,0:T(8,128)(2,1)S(1)} %collective-permute-done.23.theirs, f32[224,2048]{1,0:T(8,128)S(1)} %get-tuple-element.106.master, ...), custom_call_target="tpu_custom_call" | custom-call | flops 1 | bytes 1 | tf_op jit(solution)/shard_map/update/pallas_call | solution.py:461
  (47 shorter events, 0.3 us)
Async XLA Ops:
  0.6 12.5 %collective-permute-start.2 = (bf16[896,2048]{1,0:T(8,128)(2,1)}, bf16[896,2048]{1,0:T(8,128)(2,1)}, u32[]{:S(2)}, u32[]{:S(2)}) collective-permute-start(bf16[896,2048]{1,0:T(8,128)(2,1)} %grads.1), channel_id=1, source_target_pairs={{0,32},{32,0},{4,36},{36,4},{64,96},{96,64},{68,100},{100,68},{1,3... | collective-permute-start | bytes 11010056 | tf_op jit(solution)/shard_map/ppermute | solution.py:481
  6.9 14.9 %collective-permute-start.1 = (bf16[3,32,112,128]{3,2,1,0:T(8,128)(2,1)}, bf16[3,32,112,128]{3,2,1,0:T(8,128)(2,1)S(1)}, u32[]{:S(2)}, u32[]{:S(2)}) collective-permute-start(bf16[3,32,112,128]{3,2,1,0:T(8,128)(2,1)} %get-tuple-element.59), channel_id=1, source_target_pairs={{0,32},{32,0},{4,36},{36,4},{64,96},{96,64},{68,100},{100,68},{1,3... | collective-permute-start | bytes 8257544 | tf_op jit(solution)/shard_map/ppermute | solution.py:481
  7.1 6.0 %copy-start.5 = (s32[4]{0:T(128)S(1)}, s32[4]{0:T(128)}, u32[]{:S(2)}) copy-start(s32[4]{0:T(128)} %mixture.3) | copy-start | bytes 52
  12.6 9.7 %collective-permute-start = (bf16[4,32,112,128]{3,2,1,0:T(8,128)(2,1)}, bf16[4,32,112,128]{3,2,1,0:T(8,128)(2,1)S(1)}, u32[]{:S(2)}, u32[]{:S(2)}) collective-permute-start(bf16[4,32,112,128]{3,2,1,0:T(8,128)(2,1)} %get-tuple-element.58), channel_id=1, source_target_pairs={{0,32},{32,0},{4,36},{36,4},{64,96},{96,64},{68,100},{100,68},{1,3... | collective-permute-start | bytes 11010056 | tf_op jit(solution)/shard_map/ppermute | solution.py:481
  24.9 24.2 %collective-permute-start.3 = (bf16[16,160,256]{2,1,0:T(8,128)(2,1)S(1)}, bf16[16,160,256]{2,1,0:T(8,128)(2,1)S(1)}, u32[]{:S(2)}, u32[]{:S(2)}) collective-permute-start(bf16[16,160,256]{2,1,0:T(8,128)(2,1)S(1)} %panel_0_48_2_1.1), channel_id=1, source_target_pairs={{0,8},{32,56},{4,12},{36,60},{64,72},{96,120},{68,76},{100,124},{1... | collective-permute-start | bytes 3932168 | tf_op jit(solution)/shard_map/ppermute | solution.py:481
  29.9 23.1 %collective-permute-start.4 = (bf16[16,144,256]{2,1,0:T(8,128)(2,1)S(1)}, bf16[16,144,256]{2,1,0:T(8,128)(2,1)S(1)}, u32[]{:S(2)}, u32[]{:S(2)}) collective-permute-start(bf16[16,144,256]{2,1,0:T(8,128)(2,1)S(1)} %panel_1_48_2_1.1), channel_id=1, source_target_pairs={{0,1},{32,35},{4,5},{36,39},{64,65},{96,99},{68,69},{100,103},{1,0... | collective-permute-start | bytes 3538952 | tf_op jit(solution)/shard_map/ppermute | solution.py:481
  36.8 21.9 %collective-permute-start.5 = (bf16[16,144,256]{2,1,0:T(8,128)(2,1)S(1)}, bf16[16,144,256]{2,1,0:T(8,128)(2,1)S(1)}, u32[]{:S(2)}, u32[]{:S(2)}) collective-permute-start(bf16[16,144,256]{2,1,0:T(8,128)(2,1)S(1)} %panel_2_48_4_0.1), channel_id=1, source_target_pairs={{0,4},{32,100},{4,0},{36,96},{64,68},{96,36},{68,64},{100,32},{1,5... | collective-permute-start | bytes 3538952 | tf_op jit(solution)/shard_map/ppermute | solution.py:481
  42.7 21.7 %collective-permute-start.6 = (bf16[16,160,256]{2,1,0:T(8,128)(2,1)S(1)}, bf16[16,160,256]{2,1,0:T(8,128)(2,1)S(1)}, u32[]{:S(2)}, u32[]{:S(2)}) collective-permute-start(bf16[16,160,256]{2,1,0:T(8,128)(2,1)S(1)} %panel_0_32_4_0.1), channel_id=1, source_target_pairs={{0,8},{32,56},{4,12},{36,60},{64,72},{96,120},{68,76},{100,124},{1... | collective-permute-start | bytes 3932168 | tf_op jit(solution)/shard_map/ppermute | solution.py:481
  45.9 24.6 %collective-permute-start.7 = (bf16[16,144,256]{2,1,0:T(8,128)(2,1)S(1)}, bf16[16,144,256]{2,1,0:T(8,128)(2,1)S(1)}, u32[]{:S(2)}, u32[]{:S(2)}) collective-permute-start(bf16[16,144,256]{2,1,0:T(8,128)(2,1)S(1)} %panel_1_32_4_0.1), channel_id=1, source_target_pairs={{0,1},{32,35},{4,5},{36,39},{64,65},{96,99},{68,69},{100,103},{1,0... | collective-permute-start | bytes 3538952 | tf_op jit(solution)/shard_map/ppermute | solution.py:481
  49.1 24.5 %collective-permute-start.8 = (bf16[16,144,256]{2,1,0:T(8,128)(2,1)S(1)}, bf16[16,144,256]{2,1,0:T(8,128)(2,1)S(1)}, u32[]{:S(2)}, u32[]{:S(2)}) collective-permute-start(bf16[16,144,256]{2,1,0:T(8,128)(2,1)S(1)} %panel_2_32_4_0.1), channel_id=1, source_target_pairs={{0,4},{32,100},{4,0},{36,96},{64,68},{96,36},{68,64},{100,32},{1,5... | collective-permute-start | bytes 3538952 | tf_op jit(solution)/shard_map/ppermute | solution.py:481
  53.0 25.8 %collective-permute-start.9 = (bf16[16,160,256]{2,1,0:T(8,128)(2,1)S(1)}, bf16[16,160,256]{2,1,0:T(8,128)(2,1)S(1)}, u32[]{:S(2)}, u32[]{:S(2)}) collective-permute-start(bf16[16,160,256]{2,1,0:T(8,128)(2,1)S(1)} %panel_0_16_4_1.1), channel_id=1, source_target_pairs={{0,1},{32,35},{4,5},{36,39},{64,65},{96,99},{68,69},{100,103},{1,0... | collective-permute-start | bytes 3932168 | tf_op jit(solution)/shard_map/ppermute | solution.py:481
  58.7 20.5 %collective-permute-start.10 = (bf16[16,144,256]{2,1,0:T(8,128)(2,1)S(1)}, bf16[16,144,256]{2,1,0:T(8,128)(2,1)S(1)}, u32[]{:S(2)}, u32[]{:S(2)}) collective-permute-start(bf16[16,144,256]{2,1,0:T(8,128)(2,1)S(1)} %panel_1_16_4_1.1), channel_id=1, source_target_pairs={{0,4},{32,100},{4,0},{36,96},{64,68},{96,36},{68,64},{100,32},{1,5... | collective-permute-start | bytes 3538952 | tf_op jit(solution)/shard_map/ppermute | solution.py:481
  64.4 16.3 %collective-permute-start.11 = (bf16[16,144,256]{2,1,0:T(8,128)(2,1)S(1)}, bf16[16,144,256]{2,1,0:T(8,128)(2,1)S(1)}, u32[]{:S(2)}, u32[]{:S(2)}) collective-permute-start(bf16[16,144,256]{2,1,0:T(8,128)(2,1)S(1)} %panel_2_16_4_1.1), channel_id=1, source_target_pairs={{0,8},{32,56},{4,12},{36,60},{64,72},{96,120},{68,76},{100,124},{1... | collective-permute-start | bytes 3538952 | tf_op jit(solution)/shard_map/ppermute | solution.py:481
  70.4 13.6 %copy-start = (bf16[16,160,256]{2,1,0:T(8,128)(2,1)}, bf16[16,160,256]{2,1,0:T(8,128)(2,1)S(1)}, u32[]{:S(2)}) copy-start(bf16[16,160,256]{2,1,0:T(8,128)(2,1)S(1)} %panel_0_0_4_1.1.local) | copy-start | bytes 3932164
  73.6 10.4 %copy-start.1 = (bf16[16,144,256]{2,1,0:T(8,128)(2,1)}, bf16[16,144,256]{2,1,0:T(8,128)(2,1)S(1)}, u32[]{:S(2)}) copy-start(bf16[16,144,256]{2,1,0:T(8,128)(2,1)S(1)} %panel_1_0_4_1.1.local) | copy-start | bytes 3538948
  76.7 7.3 %copy-start.2 = (bf16[16,144,256]{2,1,0:T(8,128)(2,1)}, bf16[16,144,256]{2,1,0:T(8,128)(2,1)S(1)}, u32[]{:S(2)}) copy-start(bf16[16,144,256]{2,1,0:T(8,128)(2,1)S(1)} %panel_2_0_4_1.1.local) | copy-start | bytes 3538948
  79.0 12.3 %collective-permute-start.12 = (bf16[8,160,256]{2,1,0:T(8,128)(2,1)S(1)}, bf16[8,160,256]{2,1,0:T(8,128)(2,1)S(1)}, u32[]{:S(2)}, u32[]{:S(2)}) collective-permute-start(bf16[8,160,256]{2,1,0:T(8,128)(2,1)S(1)} %message_0.1), channel_id=1, source_target_pairs={{0,4},{32,100},{4,0},{36,96},{64,68},{96,36},{68,64},{100,32},{1,5... | collective-permute-start | bytes 1966088 | tf_op jit(solution)/shard_map/ppermute | solution.py:481
  79.2 4.8 %copy-start.3 = (bf16[16,144,256]{2,1,0:T(8,128)(2,1)}, bf16[16,144,256]{2,1,0:T(8,128)(2,1)S(1)}, u32[]{:S(2)}) copy-start(bf16[16,144,256]{2,1,0:T(8,128)(2,1)S(1)} %collective-permute-done.10.received) | copy-start | bytes 3538948
  80.7 3.3 %copy-start.4 = (bf16[16,144,256]{2,1,0:T(8,128)(2,1)}, bf16[16,144,256]{2,1,0:T(8,128)(2,1)S(1)}, u32[]{:S(2)}) copy-start(bf16[16,144,256]{2,1,0:T(8,128)(2,1)S(1)} %collective-permute-done.11.received) | copy-start | bytes 3538948
  80.9 10.0 %collective-permute-start.14 = (bf16[8,144,256]{2,1,0:T(8,128)(2,1)S(1)}, bf16[8,144,256]{2,1,0:T(8,128)(2,1)S(1)}, u32[]{:S(2)}, u32[]{:S(2)}) collective-permute-start(bf16[8,144,256]{2,1,0:T(8,128)(2,1)S(1)} %message_2.1), channel_id=1, source_target_pairs={{0,1},{32,35},{4,5},{36,39},{64,65},{96,99},{68,69},{100,103},{1,0... | collective-permute-start | bytes 1769480 | tf_op jit(solution)/shard_map/ppermute | solution.py:481
  81.3 9.9 %collective-permute-start.13 = (bf16[8,144,256]{2,1,0:T(8,128)(2,1)S(1)}, bf16[8,144,256]{2,1,0:T(8,128)(2,1)S(1)}, u32[]{:S(2)}, u32[]{:S(2)}) collective-permute-start(bf16[8,144,256]{2,1,0:T(8,128)(2,1)S(1)} %message_1.1), channel_id=1, source_target_pairs={{0,8},{32,56},{4,12},{36,60},{64,72},{96,120},{68,76},{100,124},{1... | collective-permute-start | bytes 1769480 | tf_op jit(solution)/shard_map/ppermute | solution.py:481
  84.0 1.8 %collective-permute-start.15 = (bf16[112,2048]{1,0:T(8,128)(2,1)S(1)}, bf16[112,2048]{1,0:T(8,128)(2,1)S(1)}, u32[]{:S(2)}, u32[]{:S(2)}) collective-permute-start(bf16[112,2048]{1,0:T(8,128)(2,1)S(1)} %get-tuple-element.86), channel_id=1, source_target_pairs={{0,32},{32,0},{4,36},{36,4},{64,96},{96,64},{68,100},{100,68},{1,3... | collective-permute-start | bytes 1376264 | tf_op jit(solution)/shard_map/ppermute | solution.py:481
  84.0 7.2 %slice-start = ((bf16[16,160,256]{2,1,0:T(8,128)(2,1)}), bf16[8,160,256]{2,1,0:T(8,128)(2,1)S(1)}, s32[]{:S(2)}) async-start(bf16[16,160,256]{2,1,0:T(8,128)(2,1)} %copy-done), calls=%async_computation | async-start | bytes 1310720 | tf_op jit(solution)/shard_map/slice | solution.py:562
  84.0 7.2 %slice-start.1 = ((bf16[16,144,256]{2,1,0:T(8,128)(2,1)}), bf16[8,144,256]{2,1,0:T(8,128)(2,1)S(1)}, s32[]{:S(2)}) async-start(bf16[16,144,256]{2,1,0:T(8,128)(2,1)} %copy-done.1), calls=%async_computation.1 | async-start | bytes 1179648 | tf_op jit(solution)/shard_map/slice | solution.py:562
  84.1 7.2 %slice-start.2 = ((bf16[16,144,256]{2,1,0:T(8,128)(2,1)}), bf16[8,144,256]{2,1,0:T(8,128)(2,1)S(1)}, s32[]{:S(2)}) async-start(bf16[16,144,256]{2,1,0:T(8,128)(2,1)} %copy-done.2), calls=%async_computation.2 | async-start | bytes 1179648 | tf_op jit(solution)/shard_map/slice | solution.py:562
  84.1 7.2 %slice-start.4 = ((bf16[16,144,256]{2,1,0:T(8,128)(2,1)}), bf16[8,144,256]{2,1,0:T(8,128)(2,1)S(1)}, s32[]{:S(2)}) async-start(bf16[16,144,256]{2,1,0:T(8,128)(2,1)} %copy-done.4), calls=%async_computation.4 | async-start | bytes 1179648 | tf_op jit(solution)/shard_map/slice | solution.py:562
  84.1 7.2 %slice-start.3 = ((bf16[16,144,256]{2,1,0:T(8,128)(2,1)}), bf16[8,144,256]{2,1,0:T(8,128)(2,1)S(1)}, s32[]{:S(2)}) async-start(bf16[16,144,256]{2,1,0:T(8,128)(2,1)} %copy-done.3), calls=%async_computation.3 | async-start | bytes 1179648 | tf_op jit(solution)/shard_map/slice | solution.py:562
  92.2 11.6 %collective-permute-start.16 = (bf16[2,448,256]{2,1,0:T(8,128)(2,1)S(1)}, bf16[2,448,256]{2,1,0:T(8,128)(2,1)S(1)}, u32[]{:S(2)}, u32[]{:S(2)}) collective-permute-start(bf16[2,448,256]{2,1,0:T(8,128)(2,1)S(1)} %get-tuple-element.112), channel_id=1, source_target_pairs={{0,27},{32,41},{4,31},{36,45},{64,91},{96,105},{68,95},{100,109},{... | collective-permute-start | bytes 1376264 | tf_op jit(solution)/shard_map/ppermute | solution.py:481
  92.3 11.5 %collective-permute-start.17 = (bf16[2,448,256]{2,1,0:T(8,128)(2,1)S(1)}, bf16[2,448,256]{2,1,0:T(8,128)(2,1)S(1)}, u32[]{:S(2)}, u32[]{:S(2)}) collective-permute-start(bf16[2,448,256]{2,1,0:T(8,128)(2,1)S(1)} %get-tuple-element.111), channel_id=1, source_target_pairs={{0,24},{32,40},{4,28},{36,44},{64,88},{96,104},{68,92},{100,108},{... | collective-permute-start | bytes 1376264 | tf_op jit(solution)/shard_map/ppermute | solution.py:481
  92.4 13.0 %collective-permute-start.18 = (bf16[2,448,256]{2,1,0:T(8,128)(2,1)S(1)}, bf16[2,448,256]{2,1,0:T(8,128)(2,1)S(1)}, u32[]{:S(2)}, u32[]{:S(2)}) collective-permute-start(bf16[2,448,256]{2,1,0:T(8,128)(2,1)S(1)} %get-tuple-element.110), channel_id=1, source_target_pairs={{0,3},{32,33},{4,7},{36,37},{64,67},{96,97},{68,71},{100,101},{1,2... | collective-permute-start | bytes 1376264 | tf_op jit(solution)/shard_map/ppermute | solution.py:481
  95.0 8.8 %collective-permute-start.19 = (bf16[112,1024]{1,0:T(8,128)(2,1)S(1)}, bf16[112,1024]{1,0:T(8,128)(2,1)S(1)}, u32[]{:S(2)}, u32[]{:S(2)}) collective-permute-start(bf16[112,1024]{1,0:T(8,128)(2,1)S(1)} %get-tuple-element.91), channel_id=1, source_target_pairs={{0,64},{32,96},{4,68},{36,100},{64,0},{96,32},{68,4},{100,36},{1,6... | collective-permute-start | bytes 688136 | tf_op jit(solution)/shard_map/ppermute | solution.py:481
  105.9 5.2 %collective-permute-start.20 = (bf16[448,256]{1,0:T(8,128)(2,1)S(1)}, bf16[448,256]{1,0:T(8,128)(2,1)S(1)}, u32[]{:S(2)}, u32[]{:S(2)}) collective-permute-start(bf16[448,256]{1,0:T(8,128)(2,1)S(1)} %fusion.6), channel_id=1, source_target_pairs={{0,68},{32,36},{4,64},{36,32},{64,4},{96,100},{68,0},{100,96},{1,6... | collective-permute-start | bytes 688136 | tf_op jit(solution)/shard_map/ppermute | solution.py:481
  106.0 10.2 %collective-permute-start.21 = (bf16[448,256]{1,0:T(8,128)(2,1)S(1)}, bf16[448,256]{1,0:T(8,128)(2,1)S(1)}, u32[]{:S(2)}, u32[]{:S(2)}) collective-permute-start(bf16[448,256]{1,0:T(8,128)(2,1)S(1)} %fusion.5.own), channel_id=1, source_target_pairs={{0,64},{32,96},{4,68},{36,100},{64,0},{96,32},{68,4},{100,36},{1,6... | collective-permute-start | bytes 688136 | tf_op jit(solution)/shard_map/ppermute | solution.py:481
  108.5 11.3 %collective-permute-start.22 = (bf16[448,256]{1,0:T(8,128)(2,1)S(1)}, bf16[448,256]{1,0:T(8,128)(2,1)S(1)}, u32[]{:S(2)}, u32[]{:S(2)}) collective-permute-start(bf16[448,256]{1,0:T(8,128)(2,1)S(1)} %fusion.6), channel_id=1, source_target_pairs={{0,4},{32,100},{4,0},{36,96},{64,68},{96,36},{68,64},{100,32},{1,5... | collective-permute-start | bytes 688136 | tf_op jit(solution)/shard_map/ppermute | solution.py:481
  120.5 1.9 %collective-permute-start.23 = (bf16[112,2048]{1,0:T(8,128)(2,1)S(1)}, bf16[112,2048]{1,0:T(8,128)(2,1)S(1)}, u32[]{:S(2)}, u32[]{:S(2)}) collective-permute-start(bf16[112,2048]{1,0:T(8,128)(2,1)S(1)} %combine.1.mine), channel_id=1, source_target_pairs={{0,32},{32,0},{4,36},{36,4},{64,96},{96,64},{68,100},{100,68},{1,3... | collective-permute-start | bytes 1376264 | tf_op jit(solution)/shard_map/ppermute | solution.py:481

commit v2 on v1

--- a/solution.py
+++ b/solution.py
@@ -436,45 +436,79 @@
     )(where, denominator, *sums)
 
 
-def update_kernel(where, mine, theirs, master, moment, weights_out, moment_out, weights, moments, sems):
+def updated(combined, master, moment):
+    combined = combined.astype(jnp.float32)
+    new_moment = outer_decay * moment + combined
+    return master - outer_rate * (combined + outer_decay * new_moment), new_moment
+
+
+def own_update_kernel(where, mine, master, moment, weights, moments):
     rows = mine.shape[0]
-    first = where[0] == 0
-    copies = []
-    for half in range(2):
-        here = slice(half * rows, (half + 1) * rows)
-        a, b = (mine, theirs) if half == 0 else (theirs, mine)
-        combined = jnp.where(first, a[...], b[...]).astype(jnp.float32)
-        new_moment = outer_decay * moment[here] + combined
-        new_master = master[here] - outer_rate * (combined + outer_decay * new_moment)
-        weights[here] = new_master.astype(weights.dtype)
-        moments[here] = new_moment
-        for i, (src, dst) in enumerate(((weights, weights_out), (moments, moment_out))):
-            there = pl.ds(half * rows, rows)
-            copies.append(pltpu.make_async_copy(src.at[there], dst.at[there], sems.at[half, i]))
-            copies[-1].start()
+    here = pl.ds(pl.multiple_of(where[0] * rows, 16), rows)
+    new_master, new_moment = updated(mine[...], master[here], moment[here])
+    weights[...] = new_master.astype(weights.dtype)
+    moments[...] = new_moment
+
+
+def own_update(where, mine, master, moment):
+    return pl.pallas_call(
+        own_update_kernel,
+        in_specs=[pl.BlockSpec(memory_space=pltpu.SMEM)] + [pl.BlockSpec(memory_space=pltpu.VMEM)] * 3,
+        out_specs=[pl.BlockSpec(memory_space=pltpu.VMEM)] * 2,
+        out_shape=[
+            jax.ShapeDtypeStruct(mine.shape, jnp.bfloat16),
+            jax.ShapeDtypeStruct(mine.shape, jnp.float32),
+        ],
+        compiler_params=pltpu.CompilerParams(vmem_limit_bytes=6 << 20),
+        cost_estimate=MODEST,
+        name="own_update",
+    )(where, mine, in_vmem(master), in_vmem(moment))
+
+
+def update_kernel(where, own_weights, own_moments, theirs, master, moment, weights_out, moment_out, weights, moments, sems):
+    rows = theirs.shape[0]
+    core = where[0]
+
+    def write(index, half, pair):
+        there = pl.ds(pl.multiple_of(half * rows, 16), rows)
+        return [
+            pltpu.make_async_copy(src, dst.at[there], sems.at[index, i])
+            for i, (src, dst) in enumerate(zip(pair, (weights_out, moment_out)))
+        ]
+
+    copies = write(0, core, (own_weights, own_moments))
     for copy in copies:
+        copy.start()
+    here = pl.ds(pl.multiple_of((1 - core) * rows, 16), rows)
+    new_master, new_moment = updated(theirs[...], master[here], moment[here])
+    weights[...] = new_master.astype(weights.dtype)
+    moments[...] = new_moment
+    more = write(1, 1 - core, (weights, moments))
+    for copy in more:
+        copy.start()
+    for copy in copies + more:
         copy.wait()
 
 
-def update(where, mine, theirs, master, moment):
+def update(where, own_weights, own_moments, theirs, master, moment):
     shape = master.shape
     return pl.pallas_call(
         update_kernel,
-        in_specs=[pl.BlockSpec(memory_space=pltpu.SMEM)] + [pl.BlockSpec(memory_space=pltpu.VMEM)] * 4,
+        in_specs=[pl.BlockSpec(memory_space=pltpu.SMEM)] + [pl.BlockSpec(memory_space=pltpu.VMEM)] * 5,
         out_specs=[pl.BlockSpec(memory_space=pl.ANY)] * 2,
         out_shape=[
             jax.ShapeDtypeStruct(shape, jnp.bfloat16),
             jax.ShapeDtypeStruct(shape, jnp.float32),
         ],
         scratch_shapes=[
-            pltpu.VMEM(shape, jnp.bfloat16),
-            pltpu.VMEM(shape, jnp.float32),
+            pltpu.VMEM(theirs.shape, jnp.bfloat16),
+            pltpu.VMEM(theirs.shape, jnp.float32),
             pltpu.SemaphoreType.DMA((2, 2)),
         ],
-        compiler_params=pltpu.CompilerParams(vmem_limit_bytes=10 << 20),
+        compiler_params=pltpu.CompilerParams(vmem_limit_bytes=8 << 20),
         cost_estimate=QUICK,
         name="update",
-    )(where, mine, theirs, in_vmem(master), in_vmem(moment))
+    )(where, own_weights, own_moments, theirs, in_vmem(master), in_vmem(moment))
 
 
 def send(value, pairs):
@@ -583,7 +617,9 @@
         )
     )
     half = combine(where, denominator, rows, own, own_rest, far_own, far_rest)
-    return update(where, half, send(half, swap), master, moment)
+    theirs = send(half, swap)
+    own_weights, own_moments = own_update(where, half, master, moment)
+    return update(where, own_weights, own_moments, theirs, master, moment)
 
 
 def solution(mesh):

time: 125 us -> 125 us (level)
  no operation moved by 1% of the time
where the time goes in v2:
time: 125 us
  Pallas kernels  64.6 us (52%)
  starting transfers between devices  30.2 us (24%)
  waiting for transfers between devices  26.5 us (21%)
  between operations  1.99 us (2%)
    pallas_call x14, Pallas kernels, panel(): pl.pallas_call(functools.partial(panel_kernel, first, part, tuple((offset...  40.5 us
    ppermute x24, starting transfers between devices, send(): return lax.ppermute(value, AXES, pairs)  30.2 us
    ppermute x24, waiting for transfers between devices, send(): return lax.ppermute(value, AXES, pairs)  26.5 us
    pallas_call x2, Pallas kernels, transposed(): pl.pallas_call(functools.partial(transpose_kernel, begin), in_specs=[pl.B...  10.2 us
    pallas_call x1, Pallas kernels, scaled(): pl.pallas_call(scale_kernel, in_specs=[pl.BlockSpec(memory_space=pltpu.SM...  4.33 us
  transfers between devices with their start and end apart: 24, of which 10 were waited for; matrix products, arithmetic and copies ran while one was open for 0% of the time, Pallas kernels for 47%

profile of v2, /device:TPU:1, one launch (start us, length us, event | category | flops | bytes accessed | tf_op | source)
XLA Modules:
  0.0 124.7 jit_solution(7809333610948375251)
XLA Ops:
  0.6 1.5 %collective-permute-start.2 = (bf16[896,2048]{1,0:T(8,128)(2,1)}, bf16[896,2048]{1,0:T(8,128)(2,1)}, u32[]{:S(2)}, u32[]{:S(2)}) collective-permute-start(bf16[896,2048]{1,0:T(8,128)(2,1)} %grads.1), channel_id=1, source_target_pairs={{0,32},{32,0},{4,36},{36,4},{64,96},{96,64},{68,100},{100,68},{1,3... | collective-permute-start | bytes 11010056 | tf_op jit(solution)/shard_map/ppermute | solution.py:515
  2.1 0.1 pad_add_fusion.where
  2.2 4.7 %transpose_acts_0.1 = (bf16[2,7,32,112,128]{4,3,2,1,0:T(8,128)(2,1)S(1)}, bf16[3,32,112,128]{3,2,1,0:T(8,128)(2,1)}) custom-call(s32[4]{0:T(128)S(1)} %pad_add_fusion.where, bf16[896,7168]{1,0:T(8,128)(2,1)} %acts.3), custom_call_target="tpu_custom_call" | custom-call | flops 12000000000 | bytes 1 | tf_op jit(solution)/shard_map/transpose_acts_0/pallas_call | solution.py:136
  6.9 0.2 collective-permute-start.1
  7.1 5.5 %transpose_acts_1.1 = (bf16[2,7,32,112,128]{4,3,2,1,0:T(8,128)(2,1)S(1)}, bf16[4,32,112,128]{3,2,1,0:T(8,128)(2,1)}) custom-call(s32[4]{0:T(128)S(1)} %pad_add_fusion.where, bf16[896,7168]{1,0:T(8,128)(2,1)} %acts.3, bf16[2,7,32,112,128]{4,3,2,1,0:T(8,128)(2,1)S(1)} %get-tuple-element.57.rest_0_), custom_call_target="tpu_custom_call", output_to_operand_aliasing={{0}: (2, {})} | custom-call | flops 12000000000 | bytes 1 | tf_op jit(solution)/shard_map/transpose_acts_1/pallas_call | solution.py:136
  12.6 0.5 collective-permute-start
  13.1 4.3 %scale_grads.1 = (bf16[896,2048]{1,0:T(8,128)(2,1)S(1)}, bf16[896,2048]{1,0:T(8,128)(2,1)S(1)}) custom-call(s32[4]{0:T(128)S(1)} %pad_add_fusion.where, s32[4]{0:T(128)S(1)} %copy-done.5, bf16[896,2048]{1,0:T(8,128)(2,1)} %grads.1, bf16[896,2048]{1,0:T(8,128)(2,1)} %collective-permute-done.2.other), custom_call_target="tpu_custom_call" | custom-call | flops 99999997952 | bytes 1 | tf_op jit(solution)/shard_map/scale_grads/pallas_call | solution.py:174
  17.4 2.3 %panel_0_48_2_0.1.rest_2_ = f32[16,160,256]{2,1,0:T(8,128)S(1)} custom-call(s32[4]{0:T(128)S(1)} %pad_add_fusion.where, bf16[2,7,32,112,128]{4,3,2,1,0:T(8,128)(2,1)S(1)} %get-tuple-element.64.rest_0_, bf16[896,2048]{1,0:T(8,128)(2,1)S(1)} %get-tuple-element.62.rest_1_.rest_2_), custom_call_target="tpu_custom_call" | custom-call | flops 2000000000 | bytes 1 | tf_op jit(solution)/shard_map/panel_0_48_2_0/pallas_call | solution.py:347
  19.7 2.1 %panel_1_48_2_0.1.rest_2_ = f32[16,144,256]{2,1,0:T(8,128)S(1)} custom-call(s32[4]{0:T(128)S(1)} %pad_add_fusion.where, bf16[2,7,32,112,128]{4,3,2,1,0:T(8,128)(2,1)S(1)} %get-tuple-element.64.rest_0_, bf16[896,2048]{1,0:T(8,128)(2,1)S(1)} %get-tuple-element.62.rest_1_.rest_2_), custom_call_target="tpu_custom_call" | custom-call | flops 2000000000 | bytes 1 | tf_op jit(solution)/shard_map/panel_1_48_2_0/pallas_call | solution.py:347
  21.9 0.4 load_acts_0.1.rest_0_
  22.3 0.3 load_acts_1.1.rest_0_.rest_1_
  22.5 2.3 %panel_0_48_2_1.1 = bf16[16,160,256]{2,1,0:T(8,128)(2,1)S(1)} custom-call(s32[4]{0:T(128)S(1)} %pad_add_fusion.where, bf16[7,32,112,128]{3,2,1,0:T(8,128)(2,1)S(1)} %load_acts_1.1.rest_0_.rest_1_, bf16[896,2048]{1,0:T(8,128)(2,1)S(1)} %get-tuple-element.70.rest_1_.rest_3_, f32[16,160,256]{2,1,0:T(8,128)S(1)} %panel_0_48_2_0.1.rest_2_), custom_call_target="tpu_custom_call" | custom-call | flops 2000000000 | bytes 1 | tf_op jit(solution)/shard_map/panel_0_48_2_1/pallas_call | solution.py:347
  24.8 2.9 %collective-permute-start.3 = (bf16[16,160,256]{2,1,0:T(8,128)(2,1)S(1)}, bf16[16,160,256]{2,1,0:T(8,128)(2,1)S(1)}, u32[]{:S(2)}, u32[]{:S(2)}) collective-permute-start(bf16[16,160,256]{2,1,0:T(8,128)(2,1)S(1)} %panel_0_48_2_1.1), channel_id=1, source_target_pairs={{0,8},{32,56},{4,12},{36,60},{64,72},{96,120},{68,76},{100,124},{1... | collective-permute-start | bytes 3932168 | tf_op jit(solution)/shard_map/ppermute | solution.py:515
  27.7 2.2 %panel_1_48_2_1.1 = bf16[16,144,256]{2,1,0:T(8,128)(2,1)S(1)} custom-call(s32[4]{0:T(128)S(1)} %pad_add_fusion.where, bf16[7,32,112,128]{3,2,1,0:T(8,128)(2,1)S(1)} %load_acts_1.1.rest_0_.rest_1_, bf16[896,2048]{1,0:T(8,128)(2,1)S(1)} %get-tuple-element.70.rest_1_.rest_3_, f32[16,144,256]{2,1,0:T(8,128)S(1)} %panel_1_48_2_0.1.rest_2_), custom_call_target="tpu_custom_call" | custom-call | flops 2000000000 | bytes 1 | tf_op jit(solution)/shard_map/panel_1_48_2_1/pallas_call | solution.py:347
  29.9 3.8 %collective-permute-start.4 = (bf16[16,144,256]{2,1,0:T(8,128)(2,1)S(1)}, bf16[16,144,256]{2,1,0:T(8,128)(2,1)S(1)}, u32[]{:S(2)}, u32[]{:S(2)}) collective-permute-start(bf16[16,144,256]{2,1,0:T(8,128)(2,1)S(1)} %panel_1_48_2_1.1), channel_id=1, source_target_pairs={{0,1},{32,35},{4,5},{36,39},{64,65},{96,99},{68,69},{100,103},{1,0... | collective-permute-start | bytes 3538952 | tf_op jit(solution)/shard_map/ppermute | solution.py:515
  33.7 3.1 %panel_2_48_4_0.1 = bf16[16,144,256]{2,1,0:T(8,128)(2,1)S(1)} custom-call(s32[4]{0:T(128)S(1)} %pad_add_fusion.where, bf16[2,7,32,112,128]{4,3,2,1,0:T(8,128)(2,1)S(1)} %get-tuple-element.64.rest_0_, bf16[7,32,112,128]{3,2,1,0:T(8,128)(2,1)S(1)} %load_acts_1.1.rest_0_.rest_1_, bf16[896,2048]{1,0:T(8,128)(2,1)S(1)} %get-tuple-element.62.rest_1_.rest_2_, ...), custom_call_target="tpu_custom_call" | custom-call | flops 2000000000 | bytes 1 | tf_op jit(solution)/shard_map/panel_2_48_4_0/pallas_call | solution.py:347
  36.8 2.6 %collective-permute-start.5 = (bf16[16,144,256]{2,1,0:T(8,128)(2,1)S(1)}, bf16[16,144,256]{2,1,0:T(8,128)(2,1)S(1)}, u32[]{:S(2)}, u32[]{:S(2)}) collective-permute-start(bf16[16,144,256]{2,1,0:T(8,128)(2,1)S(1)} %panel_2_48_4_0.1), channel_id=1, source_target_pairs={{0,4},{32,100},{4,0},{36,96},{64,68},{96,36},{68,64},{100,32},{1,5... | collective-permute-start | bytes 3538952 | tf_op jit(solution)/shard_map/ppermute | solution.py:515
  39.3 3.3 %panel_0_32_4_0.1 = bf16[16,160,256]{2,1,0:T(8,128)(2,1)S(1)} custom-call(s32[4]{0:T(128)S(1)} %pad_add_fusion.where, bf16[2,7,32,112,128]{4,3,2,1,0:T(8,128)(2,1)S(1)} %get-tuple-element.64.rest_0_, bf16[7,32,112,128]{3,2,1,0:T(8,128)(2,1)S(1)} %load_acts_1.1.rest_0_.rest_1_, bf16[896,2048]{1,0:T(8,128)(2,1)S(1)} %get-tuple-element.62.rest_1_.rest_2_, ...), custom_call_target="tpu_custom_call" | custom-call | flops 2000000000 | bytes 1 | tf_op jit(solution)/shard_map/panel_0_32_4_0/pallas_call | solution.py:347
  42.7 0.1 collective-permute-start.6
  42.8 3.1 %panel_1_32_4_0.1 = bf16[16,144,256]{2,1,0:T(8,128)(2,1)S(1)} custom-call(s32[4]{0:T(128)S(1)} %pad_add_fusion.where, bf16[2,7,32,112,128]{4,3,2,1,0:T(8,128)(2,1)S(1)} %get-tuple-element.64.rest_0_, bf16[7,32,112,128]{3,2,1,0:T(8,128)(2,1)S(1)} %load_acts_1.1.rest_0_.rest_1_, bf16[896,2048]{1,0:T(8,128)(2,1)S(1)} %get-tuple-element.62.rest_1_.rest_2_, ...), custom_call_target="tpu_custom_call" | custom-call | flops 2000000000 | bytes 1 | tf_op jit(solution)/shard_map/panel_1_32_4_0/pallas_call | solution.py:347
  45.9 0.2 collective-permute-start.7
  46.0 3.1 %panel_2_32_4_0.1 = bf16[16,144,256]{2,1,0:T(8,128)(2,1)S(1)} custom-call(s32[4]{0:T(128)S(1)} %pad_add_fusion.where, bf16[2,7,32,112,128]{4,3,2,1,0:T(8,128)(2,1)S(1)} %get-tuple-element.64.rest_0_, bf16[7,32,112,128]{3,2,1,0:T(8,128)(2,1)S(1)} %load_acts_1.1.rest_0_.rest_1_, bf16[896,2048]{1,0:T(8,128)(2,1)S(1)} %get-tuple-element.62.rest_1_.rest_2_, ...), custom_call_target="tpu_custom_call" | custom-call | flops 2000000000 | bytes 1 | tf_op jit(solution)/shard_map/panel_2_32_4_0/pallas_call | solution.py:347
  49.1 0.5 collective-permute-start.8
  49.6 3.4 %panel_0_16_4_1.1 = bf16[16,160,256]{2,1,0:T(8,128)(2,1)S(1)} custom-call(s32[4]{0:T(128)S(1)} %pad_add_fusion.where, bf16[2,7,32,112,128]{4,3,2,1,0:T(8,128)(2,1)S(1)} %get-tuple-element.64.rest_0_, bf16[7,32,112,128]{3,2,1,0:T(8,128)(2,1)S(1)} %load_acts_1.1.rest_0_.rest_1_, bf16[896,2048]{1,0:T(8,128)(2,1)S(1)} %get-tuple-element.62.rest_1_.rest_2_, ...), custom_call_target="tpu_custom_call" | custom-call | flops 2000000000 | bytes 1 | tf_op jit(solution)/shard_map/panel_0_16_4_1/pallas_call | solution.py:347
  53.0 2.6 %collective-permute-start.9 = (bf16[16,160,256]{2,1,0:T(8,128)(2,1)S(1)}, bf16[16,160,256]{2,1,0:T(8,128)(2,1)S(1)}, u32[]{:S(2)}, u32[]{:S(2)}) collective-permute-start(bf16[16,160,256]{2,1,0:T(8,128)(2,1)S(1)} %panel_0_16_4_1.1), channel_id=1, source_target_pairs={{0,1},{32,35},{4,5},{36,39},{64,65},{96,99},{68,69},{100,103},{1,0... | collective-permute-start | bytes 3932168 | tf_op jit(solution)/shard_map/ppermute | solution.py:515
  55.6 3.1 %panel_1_16_4_1.1 = bf16[16,144,256]{2,1,0:T(8,128)(2,1)S(1)} custom-call(s32[4]{0:T(128)S(1)} %pad_add_fusion.where, bf16[2,7,32,112,128]{4,3,2,1,0:T(8,128)(2,1)S(1)} %get-tuple-element.64.rest_0_, bf16[7,32,112,128]{3,2,1,0:T(8,128)(2,1)S(1)} %load_acts_1.1.rest_0_.rest_1_, bf16[896,2048]{1,0:T(8,128)(2,1)S(1)} %get-tuple-element.62.rest_1_.rest_2_, ...), custom_call_target="tpu_custom_call" | custom-call | flops 2000000000 | bytes 1 | tf_op jit(solution)/shard_map/panel_1_16_4_1/pallas_call | solution.py:347
  58.7 2.6 %collective-permute-start.10 = (bf16[16,144,256]{2,1,0:T(8,128)(2,1)S(1)}, bf16[16,144,256]{2,1,0:T(8,128)(2,1)S(1)}, u32[]{:S(2)}, u32[]{:S(2)}) collective-permute-start(bf16[16,144,256]{2,1,0:T(8,128)(2,1)S(1)} %panel_1_16_4_1.1), channel_id=1, source_target_pairs={{0,4},{32,100},{4,0},{36,96},{64,68},{96,36},{68,64},{100,32},{1,5... | collective-permute-start | bytes 3538952 | tf_op jit(solution)/shard_map/ppermute | solution.py:515
  61.3 3.1 %panel_2_16_4_1.1 = bf16[16,144,256]{2,1,0:T(8,128)(2,1)S(1)} custom-call(s32[4]{0:T(128)S(1)} %pad_add_fusion.where, bf16[2,7,32,112,128]{4,3,2,1,0:T(8,128)(2,1)S(1)} %get-tuple-element.64.rest_0_, bf16[7,32,112,128]{3,2,1,0:T(8,128)(2,1)S(1)} %load_acts_1.1.rest_0_.rest_1_, bf16[896,2048]{1,0:T(8,128)(2,1)S(1)} %get-tuple-element.62.rest_1_.rest_2_, ...), custom_call_target="tpu_custom_call" | custom-call | flops 2000000000 | bytes 1 | tf_op jit(solution)/shard_map/panel_2_16_4_1/pallas_call | solution.py:347
  64.4 2.7 %collective-permute-start.11 = (bf16[16,144,256]{2,1,0:T(8,128)(2,1)S(1)}, bf16[16,144,256]{2,1,0:T(8,128)(2,1)S(1)}, u32[]{:S(2)}, u32[]{:S(2)}) collective-permute-start(bf16[16,144,256]{2,1,0:T(8,128)(2,1)S(1)} %panel_2_16_4_1.1), channel_id=1, source_target_pairs={{0,8},{32,56},{4,12},{36,60},{64,72},{96,120},{68,76},{100,124},{1... | collective-permute-start | bytes 3538952 | tf_op jit(solution)/shard_map/ppermute | solution.py:515
  67.1 3.3 %panel_0_0_4_1.1.local = bf16[16,160,256]{2,1,0:T(8,128)(2,1)S(1)} custom-call(s32[4]{0:T(128)S(1)} %pad_add_fusion.where, bf16[2,7,32,112,128]{4,3,2,1,0:T(8,128)(2,1)S(1)} %get-tuple-element.64.rest_0_, bf16[7,32,112,128]{3,2,1,0:T(8,128)(2,1)S(1)} %load_acts_1.1.rest_0_.rest_1_, bf16[896,2048]{1,0:T(8,128)(2,1)S(1)} %get-tuple-element.62.rest_1_.rest_2_, ...), custom_call_target="tpu_custom_call" | custom-call | flops 2000000000 | bytes 1 | tf_op jit(solution)/shard_map/panel_0_0_4_1/pallas_call | solution.py:347
  70.5 3.1 %panel_1_0_4_1.1.local = bf16[16,144,256]{2,1,0:T(8,128)(2,1)S(1)} custom-call(s32[4]{0:T(128)S(1)} %pad_add_fusion.where, bf16[2,7,32,112,128]{4,3,2,1,0:T(8,128)(2,1)S(1)} %get-tuple-element.64.rest_0_, bf16[7,32,112,128]{3,2,1,0:T(8,128)(2,1)S(1)} %load_acts_1.1.rest_0_.rest_1_, bf16[896,2048]{1,0:T(8,128)(2,1)S(1)} %get-tuple-element.62.rest_1_.rest_2_, ...), custom_call_target="tpu_custom_call" | custom-call | flops 2000000000 | bytes 1 | tf_op jit(solution)/shard_map/panel_1_0_4_1/pallas_call | solution.py:347
  73.6 3.1 %panel_2_0_4_1.1.local = bf16[16,144,256]{2,1,0:T(8,128)(2,1)S(1)} custom-call(s32[4]{0:T(128)S(1)} %pad_add_fusion.where, bf16[2,7,32,112,128]{4,3,2,1,0:T(8,128)(2,1)S(1)} %get-tuple-element.64.rest_0_, bf16[7,32,112,128]{3,2,1,0:T(8,128)(2,1)S(1)} %load_acts_1.1.rest_0_.rest_1_, bf16[896,2048]{1,0:T(8,128)(2,1)S(1)} %get-tuple-element.62.rest_1_.rest_2_, ...), custom_call_target="tpu_custom_call" | custom-call | flops 2000000000 | bytes 1 | tf_op jit(solution)/shard_map/panel_2_0_4_1/pallas_call | solution.py:347
  76.7 2.1 %weigh_drift.1 = (f32[112,2048]{1,0:T(8,128)S(1)}, bf16[112,2048]{1,0:T(8,128)(2,1)S(1)}) custom-call(s32[4]{0:T(128)S(1)} %pad_add_fusion.where, s32[4]{0:T(128)S(1)} %copy-done.5, f32[1,224,2048]{2,1,0:T(8,128)} %drift), custom_call_target="tpu_custom_call" | custom-call | flops 1 | bytes 1 | tf_op jit(solution)/shard_map/weigh_drift/pallas_call | solution.py:226
  78.8 0.2 message_0.1
  79.0 0.3 collective-permute-start.12
  79.2 0.2 message_1.1
  79.4 1.3 %collective-permute-done.11.received = bf16[16,144,256]{2,1,0:T(8,128)(2,1)S(1)} collective-permute-done((bf16[16,144,256]{2,1,0:T(8,128)(2,1)S(1)}, bf16[16,144,256]{2,1,0:T(8,128)(2,1)S(1)}, u32[]{:S(2)}, u32[]{:S(2)}) %collective-permute-start.11) | collective-permute-done | bytes 1179680 | tf_op jit(solution)/shard_map/ppermute | solution.py:515
  80.7 0.2 message_2.1
  80.9 0.4 collective-permute-start.14
  81.3 2.7 %collective-permute-start.13 = (bf16[8,144,256]{2,1,0:T(8,128)(2,1)S(1)}, bf16[8,144,256]{2,1,0:T(8,128)(2,1)S(1)}, u32[]{:S(2)}, u32[]{:S(2)}) collective-permute-start(bf16[8,144,256]{2,1,0:T(8,128)(2,1)S(1)} %message_1.1), channel_id=1, source_target_pairs={{0,8},{32,56},{4,12},{36,60},{64,72},{96,120},{68,76},{100,124},{1... | collective-permute-start | bytes 1769480 | tf_op jit(solution)/shard_map/ppermute | solution.py:515
  84.1 1.7 %collective-permute-done.15.received = bf16[112,2048]{1,0:T(8,128)(2,1)S(1)} collective-permute-done((bf16[112,2048]{1,0:T(8,128)(2,1)S(1)}, bf16[112,2048]{1,0:T(8,128)(2,1)S(1)}, u32[]{:S(2)}, u32[]{:S(2)}) %collective-permute-start.15) | collective-permute-done | bytes 458784 | tf_op jit(solution)/shard_map/ppermute | solution.py:515
  85.8 0.7 add_drift.1
  86.5 4.4 %collective-permute-done.14 = bf16[8,144,256]{2,1,0:T(8,128)(2,1)S(1)} collective-permute-done((bf16[8,144,256]{2,1,0:T(8,128)(2,1)S(1)}, bf16[8,144,256]{2,1,0:T(8,128)(2,1)S(1)}, u32[]{:S(2)}, u32[]{:S(2)}) %collective-permute-start.14) | collective-permute-done | bytes 589856 | tf_op jit(solution)/shard_map/ppermute | solution.py:515
  90.9 0.4 collective-permute-done.13
  91.3 0.8 fusion.7
  92.1 0.1 fusion.8
  92.2 0.1 collective-permute-start.16
  92.3 0.1 collective-permute-start.17
  92.4 2.5 %collective-permute-start.18 = (bf16[2,448,256]{2,1,0:T(8,128)(2,1)S(1)}, bf16[2,448,256]{2,1,0:T(8,128)(2,1)S(1)}, u32[]{:S(2)}, u32[]{:S(2)}) collective-permute-start(bf16[2,448,256]{2,1,0:T(8,128)(2,1)S(1)} %get-tuple-element.114), channel_id=1, source_target_pairs={{0,3},{32,33},{4,7},{36,37},{64,67},{96,97},{68,71},{100,101},{1,2... | collective-permute-start | bytes 1376264 | tf_op jit(solution)/shard_map/ppermute | solution.py:515
  95.0 2.1 %load_state.1 = (f32[224,2048]{1,0:T(8,128)S(1)}, f32[224,2048]{1,0:T(8,128)S(1)}) custom-call(f32[224,2048]{1,0:T(8,128)} %master, f32[224,2048]{1,0:T(8,128)} %moment), custom_call_target="tpu_custom_call" | custom-call | flops 1 | bytes 1 | tf_op jit(solution)/shard_map/load_state/pallas_call | solution.py:392
  97.0 6.7 %collective-permute-done.19 = bf16[112,1024]{1,0:T(8,128)(2,1)S(1)} collective-permute-done((bf16[112,1024]{1,0:T(8,128)(2,1)S(1)}, bf16[112,1024]{1,0:T(8,128)(2,1)S(1)}, u32[]{:S(2)}, u32[]{:S(2)}) %collective-permute-start.19) | collective-permute-done | bytes 229408 | tf_op jit(solution)/shard_map/ppermute | solution.py:515
  103.8 1.7 %collective-permute-done.18 = bf16[2,448,256]{2,1,0:T(8,128)(2,1)S(1)} collective-permute-done((bf16[2,448,256]{2,1,0:T(8,128)(2,1)S(1)}, bf16[2,448,256]{2,1,0:T(8,128)(2,1)S(1)}, u32[]{:S(2)}, u32[]{:S(2)}) %collective-permute-start.18) | collective-permute-done | bytes 458784 | tf_op jit(solution)/shard_map/ppermute | solution.py:515
  105.6 0.2 fusion.1
  105.9 0.1 collective-permute-start.20
  106.0 2.5 %collective-permute-start.21 = (bf16[448,256]{1,0:T(8,128)(2,1)S(1)}, bf16[448,256]{1,0:T(8,128)(2,1)S(1)}, u32[]{:S(2)}, u32[]{:S(2)}) collective-permute-start(bf16[448,256]{1,0:T(8,128)(2,1)S(1)} %fusion.5.own), channel_id=1, source_target_pairs={{0,64},{32,96},{4,68},{36,100},{64,0},{96,32},{68,4},{100,36},{1,6... | collective-permute-start | bytes 688136 | tf_op jit(solution)/shard_map/ppermute | solution.py:515
  108.5 1.4 %collective-permute-start.22 = (bf16[448,256]{1,0:T(8,128)(2,1)S(1)}, bf16[448,256]{1,0:T(8,128)(2,1)S(1)}, u32[]{:S(2)}, u32[]{:S(2)}) collective-permute-start(bf16[448,256]{1,0:T(8,128)(2,1)S(1)} %fusion.6), channel_id=1, source_target_pairs={{0,4},{32,100},{4,0},{36,96},{64,68},{96,36},{68,64},{100,32},{1,5... | collective-permute-start | bytes 688136 | tf_op jit(solution)/shard_map/ppermute | solution.py:515
  110.5 0.7 collective-permute-done.20.own_rest
  111.2 5.0 %collective-permute-done.21.far_own = bf16[448,256]{1,0:T(8,128)(2,1)S(1)} collective-permute-done((bf16[448,256]{1,0:T(8,128)(2,1)S(1)}, bf16[448,256]{1,0:T(8,128)(2,1)S(1)}, u32[]{:S(2)}, u32[]{:S(2)}) %collective-permute-start.21) | collective-permute-done | bytes 229408 | tf_op jit(solution)/shard_map/ppermute | solution.py:515
  116.2 3.6 %collective-permute-done.22.far_rest = bf16[448,256]{1,0:T(8,128)(2,1)S(1)} collective-permute-done((bf16[448,256]{1,0:T(8,128)(2,1)S(1)}, bf16[448,256]{1,0:T(8,128)(2,1)S(1)}, u32[]{:S(2)}, u32[]{:S(2)}) %collective-permute-start.22) | collective-permute-done | bytes 229408 | tf_op jit(solution)/shard_map/ppermute | solution.py:515
  119.8 0.7 combine.1.mine
  120.5 0.1 collective-permute-start.23
  120.6 0.8 own_update.1
  121.4 1.0 collective-permute-done.23.theirs
  122.4 2.1 %update.1 = (bf16[224,2048]{1,0:T(8,128)(2,1)}, f32[224,2048]{1,0:T(8,128)}) custom-call(s32[4]{0:T(128)S(1)} %pad_add_fusion.where, bf16[112,2048]{1,0:T(8,128)(2,1)S(1)} %get-tuple-element.110.own_weights, f32[112,2048]{1,0:T(8,128)S(1)} %get-tuple-element.111.own_moments, bf16[112,2048]{1,0:T(8,128)(2,1)S(1)} %collective-permute-done.23.theirs, ...), custom_call_target="tpu_custom_call" | custom-call | flops 1 | bytes 1 | tf_op jit(solution)/shard_map/update/pallas_call | solution.py:495
  (48 shorter events, 0.3 us)
Async XLA Ops:
  0.6 12.5 %collective-permute-start.2 = (bf16[896,2048]{1,0:T(8,128)(2,1)}, bf16[896,2048]{1,0:T(8,128)(2,1)}, u32[]{:S(2)}, u32[]{:S(2)}) collective-permute-start(bf16[896,2048]{1,0:T(8,128)(2,1)} %grads.1), channel_id=1, source_target_pairs={{0,32},{32,0},{4,36},{36,4},{64,96},{96,64},{68,100},{100,68},{1,3... | collective-permute-start | bytes 11010056 | tf_op jit(solution)/shard_map/ppermute | solution.py:515
  6.9 14.9 %collective-permute-start.1 = (bf16[3,32,112,128]{3,2,1,0:T(8,128)(2,1)}, bf16[3,32,112,128]{3,2,1,0:T(8,128)(2,1)S(1)}, u32[]{:S(2)}, u32[]{:S(2)}) collective-permute-start(bf16[3,32,112,128]{3,2,1,0:T(8,128)(2,1)} %get-tuple-element.61), channel_id=1, source_target_pairs={{0,32},{32,0},{4,36},{36,4},{64,96},{96,64},{68,100},{100,68},{1,3... | collective-permute-start | bytes 8257544 | tf_op jit(solution)/shard_map/ppermute | solution.py:515
  7.1 6.0 %copy-start.5 = (s32[4]{0:T(128)S(1)}, s32[4]{0:T(128)}, u32[]{:S(2)}) copy-start(s32[4]{0:T(128)} %mixture.3) | copy-start | bytes 52
  12.6 9.7 %collective-permute-start = (bf16[4,32,112,128]{3,2,1,0:T(8,128)(2,1)}, bf16[4,32,112,128]{3,2,1,0:T(8,128)(2,1)S(1)}, u32[]{:S(2)}, u32[]{:S(2)}) collective-permute-start(bf16[4,32,112,128]{3,2,1,0:T(8,128)(2,1)} %get-tuple-element.60), channel_id=1, source_target_pairs={{0,32},{32,0},{4,36},{36,4},{64,96},{96,64},{68,100},{100,68},{1,3... | collective-permute-start | bytes 11010056 | tf_op jit(solution)/shard_map/ppermute | solution.py:515
  24.8 24.2 %collective-permute-start.3 = (bf16[16,160,256]{2,1,0:T(8,128)(2,1)S(1)}, bf16[16,160,256]{2,1,0:T(8,128)(2,1)S(1)}, u32[]{:S(2)}, u32[]{:S(2)}) collective-permute-start(bf16[16,160,256]{2,1,0:T(8,128)(2,1)S(1)} %panel_0_48_2_1.1), channel_id=1, source_target_pairs={{0,8},{32,56},{4,12},{36,60},{64,72},{96,120},{68,76},{100,124},{1... | collective-permute-start | bytes 3932168 | tf_op jit(solution)/shard_map/ppermute | solution.py:515
  29.9 23.0 %collective-permute-start.4 = (bf16[16,144,256]{2,1,0:T(8,128)(2,1)S(1)}, bf16[16,144,256]{2,1,0:T(8,128)(2,1)S(1)}, u32[]{:S(2)}, u32[]{:S(2)}) collective-permute-start(bf16[16,144,256]{2,1,0:T(8,128)(2,1)S(1)} %panel_1_48_2_1.1), channel_id=1, source_target_pairs={{0,1},{32,35},{4,5},{36,39},{64,65},{96,99},{68,69},{100,103},{1,0... | collective-permute-start | bytes 3538952 | tf_op jit(solution)/shard_map/ppermute | solution.py:515
  36.8 21.9 %collective-permute-start.5 = (bf16[16,144,256]{2,1,0:T(8,128)(2,1)S(1)}, bf16[16,144,256]{2,1,0:T(8,128)(2,1)S(1)}, u32[]{:S(2)}, u32[]{:S(2)}) collective-permute-start(bf16[16,144,256]{2,1,0:T(8,128)(2,1)S(1)} %panel_2_48_4_0.1), channel_id=1, source_target_pairs={{0,4},{32,100},{4,0},{36,96},{64,68},{96,36},{68,64},{100,32},{1,5... | collective-permute-start | bytes 3538952 | tf_op jit(solution)/shard_map/ppermute | solution.py:515
  42.7 21.7 %collective-permute-start.6 = (bf16[16,160,256]{2,1,0:T(8,128)(2,1)S(1)}, bf16[16,160,256]{2,1,0:T(8,128)(2,1)S(1)}, u32[]{:S(2)}, u32[]{:S(2)}) collective-permute-start(bf16[16,160,256]{2,1,0:T(8,128)(2,1)S(1)} %panel_0_32_4_0.1), channel_id=1, source_target_pairs={{0,8},{32,56},{4,12},{36,60},{64,72},{96,120},{68,76},{100,124},{1... | collective-permute-start | bytes 3932168 | tf_op jit(solution)/shard_map/ppermute | solution.py:515
  45.9 24.6 %collective-permute-start.7 = (bf16[16,144,256]{2,1,0:T(8,128)(2,1)S(1)}, bf16[16,144,256]{2,1,0:T(8,128)(2,1)S(1)}, u32[]{:S(2)}, u32[]{:S(2)}) collective-permute-start(bf16[16,144,256]{2,1,0:T(8,128)(2,1)S(1)} %panel_1_32_4_0.1), channel_id=1, source_target_pairs={{0,1},{32,35},{4,5},{36,39},{64,65},{96,99},{68,69},{100,103},{1,0... | collective-permute-start | bytes 3538952 | tf_op jit(solution)/shard_map/ppermute | solution.py:515
  49.1 24.5 %collective-permute-start.8 = (bf16[16,144,256]{2,1,0:T(8,128)(2,1)S(1)}, bf16[16,144,256]{2,1,0:T(8,128)(2,1)S(1)}, u32[]{:S(2)}, u32[]{:S(2)}) collective-permute-start(bf16[16,144,256]{2,1,0:T(8,128)(2,1)S(1)} %panel_2_32_4_0.1), channel_id=1, source_target_pairs={{0,4},{32,100},{4,0},{36,96},{64,68},{96,36},{68,64},{100,32},{1,5... | collective-permute-start | bytes 3538952 | tf_op jit(solution)/shard_map/ppermute | solution.py:515
  53.0 25.8 %collective-permute-start.9 = (bf16[16,160,256]{2,1,0:T(8,128)(2,1)S(1)}, bf16[16,160,256]{2,1,0:T(8,128)(2,1)S(1)}, u32[]{:S(2)}, u32[]{:S(2)}) collective-permute-start(bf16[16,160,256]{2,1,0:T(8,128)(2,1)S(1)} %panel_0_16_4_1.1), channel_id=1, source_target_pairs={{0,1},{32,35},{4,5},{36,39},{64,65},{96,99},{68,69},{100,103},{1,0... | collective-permute-start | bytes 3932168 | tf_op jit(solution)/shard_map/ppermute | solution.py:515
  58.7 20.5 %collective-permute-start.10 = (bf16[16,144,256]{2,1,0:T(8,128)(2,1)S(1)}, bf16[16,144,256]{2,1,0:T(8,128)(2,1)S(1)}, u32[]{:S(2)}, u32[]{:S(2)}) collective-permute-start(bf16[16,144,256]{2,1,0:T(8,128)(2,1)S(1)} %panel_1_16_4_1.1), channel_id=1, source_target_pairs={{0,4},{32,100},{4,0},{36,96},{64,68},{96,36},{68,64},{100,32},{1,5... | collective-permute-start | bytes 3538952 | tf_op jit(solution)/shard_map/ppermute | solution.py:515
  64.4 16.3 %collective-permute-start.11 = (bf16[16,144,256]{2,1,0:T(8,128)(2,1)S(1)}, bf16[16,144,256]{2,1,0:T(8,128)(2,1)S(1)}, u32[]{:S(2)}, u32[]{:S(2)}) collective-permute-start(bf16[16,144,256]{2,1,0:T(8,128)(2,1)S(1)} %panel_2_16_4_1.1), channel_id=1, source_target_pairs={{0,8},{32,56},{4,12},{36,60},{64,72},{96,120},{68,76},{100,124},{1... | collective-permute-start | bytes 3538952 | tf_op jit(solution)/shard_map/ppermute | solution.py:515
  70.4 13.6 %copy-start = (bf16[16,160,256]{2,1,0:T(8,128)(2,1)}, bf16[16,160,256]{2,1,0:T(8,128)(2,1)S(1)}, u32[]{:S(2)}) copy-start(bf16[16,160,256]{2,1,0:T(8,128)(2,1)S(1)} %panel_0_0_4_1.1.local) | copy-start | bytes 3932164
  73.6 10.4 %copy-start.1 = (bf16[16,144,256]{2,1,0:T(8,128)(2,1)}, bf16[16,144,256]{2,1,0:T(8,128)(2,1)S(1)}, u32[]{:S(2)}) copy-start(bf16[16,144,256]{2,1,0:T(8,128)(2,1)S(1)} %panel_1_0_4_1.1.local) | copy-start | bytes 3538948
  76.7 7.3 %copy-start.2 = (bf16[16,144,256]{2,1,0:T(8,128)(2,1)}, bf16[16,144,256]{2,1,0:T(8,128)(2,1)S(1)}, u32[]{:S(2)}) copy-start(bf16[16,144,256]{2,1,0:T(8,128)(2,1)S(1)} %panel_2_0_4_1.1.local) | copy-start | bytes 3538948
  79.0 12.3 %collective-permute-start.12 = (bf16[8,160,256]{2,1,0:T(8,128)(2,1)S(1)}, bf16[8,160,256]{2,1,0:T(8,128)(2,1)S(1)}, u32[]{:S(2)}, u32[]{:S(2)}) collective-permute-start(bf16[8,160,256]{2,1,0:T(8,128)(2,1)S(1)} %message_0.1), channel_id=1, source_target_pairs={{0,4},{32,100},{4,0},{36,96},{64,68},{96,36},{68,64},{100,32},{1,5... | collective-permute-start | bytes 1966088 | tf_op jit(solution)/shard_map/ppermute | solution.py:515
  79.2 4.8 %copy-start.3 = (bf16[16,144,256]{2,1,0:T(8,128)(2,1)}, bf16[16,144,256]{2,1,0:T(8,128)(2,1)S(1)}, u32[]{:S(2)}) copy-start(bf16[16,144,256]{2,1,0:T(8,128)(2,1)S(1)} %collective-permute-done.10.received) | copy-start | bytes 3538948
  80.7 3.3 %copy-start.4 = (bf16[16,144,256]{2,1,0:T(8,128)(2,1)}, bf16[16,144,256]{2,1,0:T(8,128)(2,1)S(1)}, u32[]{:S(2)}) copy-start(bf16[16,144,256]{2,1,0:T(8,128)(2,1)S(1)} %collective-permute-done.11.received) | copy-start | bytes 3538948
  80.9 10.0 %collective-permute-start.14 = (bf16[8,144,256]{2,1,0:T(8,128)(2,1)S(1)}, bf16[8,144,256]{2,1,0:T(8,128)(2,1)S(1)}, u32[]{:S(2)}, u32[]{:S(2)}) collective-permute-start(bf16[8,144,256]{2,1,0:T(8,128)(2,1)S(1)} %message_2.1), channel_id=1, source_target_pairs={{0,1},{32,35},{4,5},{36,39},{64,65},{96,99},{68,69},{100,103},{1,0... | collective-permute-start | bytes 1769480 | tf_op jit(solution)/shard_map/ppermute | solution.py:515
  81.3 9.9 %collective-permute-start.13 = (bf16[8,144,256]{2,1,0:T(8,128)(2,1)S(1)}, bf16[8,144,256]{2,1,0:T(8,128)(2,1)S(1)}, u32[]{:S(2)}, u32[]{:S(2)}) collective-permute-start(bf16[8,144,256]{2,1,0:T(8,128)(2,1)S(1)} %message_1.1), channel_id=1, source_target_pairs={{0,8},{32,56},{4,12},{36,60},{64,72},{96,120},{68,76},{100,124},{1... | collective-permute-start | bytes 1769480 | tf_op jit(solution)/shard_map/ppermute | solution.py:515
  84.0 1.8 %collective-permute-start.15 = (bf16[112,2048]{1,0:T(8,128)(2,1)S(1)}, bf16[112,2048]{1,0:T(8,128)(2,1)S(1)}, u32[]{:S(2)}, u32[]{:S(2)}) collective-permute-start(bf16[112,2048]{1,0:T(8,128)(2,1)S(1)} %get-tuple-element.88), channel_id=1, source_target_pairs={{0,32},{32,0},{4,36},{36,4},{64,96},{96,64},{68,100},{100,68},{1,3... | collective-permute-start | bytes 1376264 | tf_op jit(solution)/shard_map/ppermute | solution.py:515
  84.0 7.3 %slice-start = ((bf16[16,160,256]{2,1,0:T(8,128)(2,1)}), bf16[8,160,256]{2,1,0:T(8,128)(2,1)S(1)}, s32[]{:S(2)}) async-start(bf16[16,160,256]{2,1,0:T(8,128)(2,1)} %copy-done), calls=%async_computation | async-start | bytes 1310720 | tf_op jit(solution)/shard_map/slice | solution.py:596
  84.0 7.2 %slice-start.1 = ((bf16[16,144,256]{2,1,0:T(8,128)(2,1)}), bf16[8,144,256]{2,1,0:T(8,128)(2,1)S(1)}, s32[]{:S(2)}) async-start(bf16[16,144,256]{2,1,0:T(8,128)(2,1)} %copy-done.1), calls=%async_computation.1 | async-start | bytes 1179648 | tf_op jit(solution)/shard_map/slice | solution.py:596
  84.1 7.2 %slice-start.2 = ((bf16[16,144,256]{2,1,0:T(8,128)(2,1)}), bf16[8,144,256]{2,1,0:T(8,128)(2,1)S(1)}, s32[]{:S(2)}) async-start(bf16[16,144,256]{2,1,0:T(8,128)(2,1)} %copy-done.2), calls=%async_computation.2 | async-start | bytes 1179648 | tf_op jit(solution)/shard_map/slice | solution.py:596
  84.1 7.2 %slice-start.4 = ((bf16[16,144,256]{2,1,0:T(8,128)(2,1)}), bf16[8,144,256]{2,1,0:T(8,128)(2,1)S(1)}, s32[]{:S(2)}) async-start(bf16[16,144,256]{2,1,0:T(8,128)(2,1)} %copy-done.4), calls=%async_computation.4 | async-start | bytes 1179648 | tf_op jit(solution)/shard_map/slice | solution.py:596
  84.1 7.2 %slice-start.3 = ((bf16[16,144,256]{2,1,0:T(8,128)(2,1)}), bf16[8,144,256]{2,1,0:T(8,128)(2,1)S(1)}, s32[]{:S(2)}) async-start(bf16[16,144,256]{2,1,0:T(8,128)(2,1)} %copy-done.3), calls=%async_computation.3 | async-start | bytes 1179648 | tf_op jit(solution)/shard_map/slice | solution.py:596
  92.2 11.5 %collective-permute-start.16 = (bf16[2,448,256]{2,1,0:T(8,128)(2,1)S(1)}, bf16[2,448,256]{2,1,0:T(8,128)(2,1)S(1)}, u32[]{:S(2)}, u32[]{:S(2)}) collective-permute-start(bf16[2,448,256]{2,1,0:T(8,128)(2,1)S(1)} %get-tuple-element.116), channel_id=1, source_target_pairs={{0,27},{32,41},{4,31},{36,45},{64,91},{96,105},{68,95},{100,109},{... | collective-permute-start | bytes 1376264 | tf_op jit(solution)/shard_map/ppermute | solution.py:515
  92.3 11.5 %collective-permute-start.17 = (bf16[2,448,256]{2,1,0:T(8,128)(2,1)S(1)}, bf16[2,448,256]{2,1,0:T(8,128)(2,1)S(1)}, u32[]{:S(2)}, u32[]{:S(2)}) collective-permute-start(bf16[2,448,256]{2,1,0:T(8,128)(2,1)S(1)} %get-tuple-element.115), channel_id=1, source_target_pairs={{0,24},{32,40},{4,28},{36,44},{64,88},{96,104},{68,92},{100,108},{... | collective-permute-start | bytes 1376264 | tf_op jit(solution)/shard_map/ppermute | solution.py:515
  92.4 13.0 %collective-permute-start.18 = (bf16[2,448,256]{2,1,0:T(8,128)(2,1)S(1)}, bf16[2,448,256]{2,1,0:T(8,128)(2,1)S(1)}, u32[]{:S(2)}, u32[]{:S(2)}) collective-permute-start(bf16[2,448,256]{2,1,0:T(8,128)(2,1)S(1)} %get-tuple-element.114), channel_id=1, source_target_pairs={{0,3},{32,33},{4,7},{36,37},{64,67},{96,97},{68,71},{100,101},{1,2... | collective-permute-start | bytes 1376264 | tf_op jit(solution)/shard_map/ppermute | solution.py:515
  95.0 8.8 %collective-permute-start.19 = (bf16[112,1024]{1,0:T(8,128)(2,1)S(1)}, bf16[112,1024]{1,0:T(8,128)(2,1)S(1)}, u32[]{:S(2)}, u32[]{:S(2)}) collective-permute-start(bf16[112,1024]{1,0:T(8,128)(2,1)S(1)} %get-tuple-element.93), channel_id=1, source_target_pairs={{0,64},{32,96},{4,68},{36,100},{64,0},{96,32},{68,4},{100,36},{1,6... | collective-permute-start | bytes 688136 | tf_op jit(solution)/shard_map/ppermute | solution.py:515
  105.9 5.2 %collective-permute-start.20 = (bf16[448,256]{1,0:T(8,128)(2,1)S(1)}, bf16[448,256]{1,0:T(8,128)(2,1)S(1)}, u32[]{:S(2)}, u32[]{:S(2)}) collective-permute-start(bf16[448,256]{1,0:T(8,128)(2,1)S(1)} %fusion.6), channel_id=1, source_target_pairs={{0,68},{32,36},{4,64},{36,32},{64,4},{96,100},{68,0},{100,96},{1,6... | collective-permute-start | bytes 688136 | tf_op jit(solution)/shard_map/ppermute | solution.py:515
  106.0 10.2 %collective-permute-start.21 = (bf16[448,256]{1,0:T(8,128)(2,1)S(1)}, bf16[448,256]{1,0:T(8,128)(2,1)S(1)}, u32[]{:S(2)}, u32[]{:S(2)}) collective-permute-start(bf16[448,256]{1,0:T(8,128)(2,1)S(1)} %fusion.5.own), channel_id=1, source_target_pairs={{0,64},{32,96},{4,68},{36,100},{64,0},{96,32},{68,4},{100,36},{1,6... | collective-permute-start | bytes 688136 | tf_op jit(solution)/shard_map/ppermute | solution.py:515
  108.5 11.3 %collective-permute-start.22 = (bf16[448,256]{1,0:T(8,128)(2,1)S(1)}, bf16[448,256]{1,0:T(8,128)(2,1)S(1)}, u32[]{:S(2)}, u32[]{:S(2)}) collective-permute-start(bf16[448,256]{1,0:T(8,128)(2,1)S(1)} %fusion.6), channel_id=1, source_target_pairs={{0,4},{32,100},{4,0},{36,96},{64,68},{96,36},{68,64},{100,32},{1,5... | collective-permute-start | bytes 688136 | tf_op jit(solution)/shard_map/ppermute | solution.py:515
  120.5 1.9 %collective-permute-start.23 = (bf16[112,2048]{1,0:T(8,128)(2,1)S(1)}, bf16[112,2048]{1,0:T(8,128)(2,1)S(1)}, u32[]{:S(2)}, u32[]{:S(2)}) collective-permute-start(bf16[112,2048]{1,0:T(8,128)(2,1)S(1)} %combine.1.mine), channel_id=1, source_target_pairs={{0,32},{32,0},{4,36},{36,4},{64,96},{96,64},{68,100},{100,68},{1,3... | collective-permute-start | bytes 1376264 | tf_op jit(solution)/shard_map/ppermute | solution.py:515
